TPU v7x, 128 devices: a whole 4x4x4 slice. The times are simulated.
128 devices in a mesh: row: 8 (over x, core), col: 16 (over y, z).
Axes of the slice: x: 4, y: 4, z: 4, core: 2. Of those that a mesh axis runs over, the one named last changes fastest.
Arguments:
- density: float32 [128, 128, 8192], P('row', 'col'), may hold values from -6 to 6
- integrals: bfloat16 [1024, 1024, 1024], P(('row', 'col')), may hold values from -0.046875 to 0.046875
- quartets: int32 [992, 4], replicated, may hold values from 0 to 127
- holder: int32 [992], replicated, may hold values from 0 to 127, as said below
- degeneracy: int32 [992], replicated, may hold values from 1 to 8, as said below
Outputs:
- fock: float32 [128, 128, 8192], P('row', 'col')
Inputs may be any that keep to these rules, and one draw needn't show every extreme that they name: `holder`: each device holds at most 8 quartets and some device holds exactly 8; the six blocks (p,q), (r,s), (p,r), (p,s), (q,r), (q,s) of all quartets on one device have pairwise different owners, the owner of block (a, b) being the device at row a // (128 / 8) and col b // (128 / 16). `degeneracy`: powers of two.
All inputs are finite; a program needn't handle non-finite values.
Results may differ from a plain program's by a relative error of at most 0.0029.
Values may be sent and summed in bfloat16 or wider, within the bound.
A program may use at most 256 MiB of HBM per device.

v0:
```python
import jax
import jax.numpy as jnp
from jax import lax
from jax.sharding import PartitionSpec as P

BS = 32
PERT = 8


def quartet_terms(block, pair_dens, factor):
    four = block.reshape(BS, BS, BS, BS)
    d_pq, d_rs, d_pr, d_ps, d_qr, d_qs = pair_dens
    f32 = jnp.float32
    j_pq = jnp.einsum("pqrs,krs->kpq", four, d_rs, preferred_element_type=f32)
    j_rs = jnp.einsum("pqrs,kpq->krs", four, d_pq, preferred_element_type=f32)
    k_pr = jnp.einsum("pqrs,kqs->kpr", four, d_qs, preferred_element_type=f32)
    k_ps = jnp.einsum("pqrs,kqr->kps", four, d_qr, preferred_element_type=f32)
    k_qr = jnp.einsum("pqrs,kps->kqr", four, d_ps, preferred_element_type=f32)
    k_qs = jnp.einsum("pqrs,kpr->kqs", four, d_pr, preferred_element_type=f32)
    coul = 2.0 * factor
    exch = -0.5 * factor
    return [coul * j_pq, coul * j_rs, exch * k_pr, exch * k_ps, exch * k_qr, exch * k_qs]


def local(density, integrals, quartets, holder, degeneracy):
    row_count = lax.axis_size("row")
    col_count = lax.axis_size("col")
    devices_all = row_count * col_count
    self_id = lax.axis_index("row") * col_count + lax.axis_index("col")
    local_rows = density.shape[0]
    local_cols = density.shape[1]
    row_start = lax.axis_index("row") * local_rows
    col_start = lax.axis_index("col") * local_cols
    local_count = local_rows * local_cols
    flat_blocks = density.reshape(local_count, density.shape[2]).astype(jnp.bfloat16)
    count = holder.shape[0]
    first_idx = jnp.stack(
        [
            quartets[:, 0],
            quartets[:, 2],
            quartets[:, 0],
            quartets[:, 0],
            quartets[:, 1],
            quartets[:, 1],
        ],
        1,
    )
    second_idx = jnp.stack(
        [
            quartets[:, 1],
            quartets[:, 3],
            quartets[:, 2],
            quartets[:, 3],
            quartets[:, 2],
            quartets[:, 3],
        ],
        1,
    )
    owner_dev = first_idx // local_rows * col_count + second_idx // local_cols
    local_id = (first_idx - row_start) * local_cols + (second_idx - col_start)
    dest_dev = jnp.where(owner_dev == self_id, holder[:, None], devices_all).reshape(-1)
    send_table = (
        jnp.zeros((devices_all,), jnp.int32).at[dest_dev].set(local_id.reshape(-1), mode="drop")
    )
    present = jnp.zeros((devices_all,), jnp.bool_).at[dest_dev].set(True, mode="drop")
    outgoing = jnp.where(present[:, None], flat_blocks[send_table], jnp.zeros((), jnp.bfloat16))
    incoming = lax.all_to_all(outgoing, ("row", "col"), split_axis=0, concat_axis=0, tiled=True)
    order = jnp.arange(count, dtype=jnp.int32)
    earlier = (holder[None, :] == holder[:, None]) & (order[None, :] < order[:, None])
    slot_rank = jnp.sum(earlier.astype(jnp.int32), axis=1)
    returned = jnp.zeros(outgoing.shape, jnp.float32)
    for slot_j in range(integrals.shape[0]):
        match = (holder == self_id) & (slot_rank == slot_j)
        is_live = jnp.any(match)
        chosen = jnp.argmax(match.astype(jnp.int32))
        owners_six = owner_dev[chosen]
        factor = degeneracy[chosen].astype(jnp.float32) * is_live.astype(jnp.float32)
        fetched = incoming[owners_six].reshape(6, PERT, BS, BS)
        terms = quartet_terms(integrals[slot_j], [fetched[t] for t in range(6)], factor)
        stacked = jnp.stack([terms[t].reshape(-1) for t in range(6)], 0)
        returned = returned.at[owners_six].add(stacked)
    arrived = lax.all_to_all(returned, ("row", "col"), split_axis=0, concat_axis=0, tiled=True)
    target_id = jnp.where(present, send_table, local_count)
    fock_flat = jnp.zeros(flat_blocks.shape, jnp.float32).at[target_id].add(arrived, mode="drop")
    return fock_flat.reshape(density.shape)


def solution(mesh):
    return jax.shard_map(
        local,
        mesh=mesh,
        in_specs=(P("row", "col", None), P(("row", "col"), None, None), P(), P(), P()),
        out_specs=P("row", "col", None),
        check_vma=False,
    )
```

profile of v0, /device:TPU:1, one launch (start us, length us, event | category | flops | bytes accessed | tf_op | source)
XLA Modules:
  0.0 690.0 jit_solution(6266907738740374035)
XLA Ops:
  5.1 28.7 %scatter_custom_fusion.1 = s32[128]{0:T(128)S(1)} fusion(s32[5952]{0:T(1024)S(1)} %fusion.269, s32[5952]{0:T(1024)S(1)} %reshape.639, s32[]{:T(128)} %constant.81.clone.1), kind=kCustom, calls=%fused_computation.387 | custom fusion | bytes 516 | tf_op jit(solution)/shard_map/scatter | solution.py:63
  33.9 32.6 %scatter_custom_fusion = pred[128]{0:T(512)(128)(4,1)S(1)} fusion(s32[5952]{0:T(1024)S(1)} %fusion.269, pred[5952]{0:T(1024)(128)(4,1)S(1)} %broadcast.333, pred[]{:T(512)} %constant.79.clone.1), kind=kCustom, calls=%fused_computation.377 | custom fusion | bytes 129 | tf_op jit(solution)/shard_map/scatter | solution.py:65
  82.5 12.0 %all-to-all-start = ((bf16[128,2,4096]{2,1,0:T(2,128)(2,1)}), bf16[128,2,4096]{2,1,0:T(2,128)(2,1)}, u32[]{:S(2)}, u32[]{:S(2)}) async-start(bf16[128,2,4096]{2,1,0:T(2,128)(2,1)} %reshape.878), calls=%async_computation | async-start | bytes 4194304 | tf_op jit(solution)/shard_map/all_to_all | solution.py:67
  100.4 11.4 %fusion.290 = (bf16[1,1024,1024]{2,1,0:T(8,128)(2,1)}, bf16[1,1024,1024]{2,1,0:T(8,128)(2,1)}, bf16[1,1024,1024]{2,1,0:T(8,128)(2,1)}, bf16[1,1024,1024]{2,1,0:T...) fusion(bf16[8,1024,1024]{2,1,0:T(8,128)(2,1)} %param.6), kind=kLoop, calls=%fused_computation.397 | loop fusion | bytes 33554432 | tf_op jit(solution)/shard_map/slice | solution.py:79
  138.2 10.9 %reshape_squeeze.31 = bf16[32,32,32,32]{3,2,1,0:T(8,128)(2,1)} reshape(bf16[1,1024,1024]{2,1,0:T(8,128)(2,1)} %get-tuple-element.94) | data formatting | bytes 4194304 | tf_op jit(solution)/shard_map/reshape;squeeze | solution.py:11
  149.1 10.9 %reshape_squeeze.30 = bf16[32,32,32,32]{3,2,1,0:T(8,128)(2,1)} reshape(bf16[1,1024,1024]{2,1,0:T(8,128)(2,1)} %get-tuple-element.101) | data formatting | bytes 4194304 | tf_op jit(solution)/shard_map/reshape;squeeze | solution.py:11
  160.0 10.9 %reshape_squeeze.29 = bf16[32,32,32,32]{3,2,1,0:T(8,128)(2,1)} reshape(bf16[1,1024,1024]{2,1,0:T(8,128)(2,1)} %get-tuple-element.95) | data formatting | bytes 4194304 | tf_op jit(solution)/shard_map/reshape;squeeze | solution.py:11
  170.9 10.9 %reshape_squeeze.28 = bf16[32,32,32,32]{3,2,1,0:T(8,128)(2,1)} reshape(bf16[1,1024,1024]{2,1,0:T(8,128)(2,1)} %get-tuple-element.96) | data formatting | bytes 4194304 | tf_op jit(solution)/shard_map/reshape;squeeze | solution.py:11
  181.8 10.9 %reshape_squeeze.27 = bf16[32,32,32,32]{3,2,1,0:T(8,128)(2,1)} reshape(bf16[1,1024,1024]{2,1,0:T(8,128)(2,1)} %get-tuple-element.97) | data formatting | bytes 4194304 | tf_op jit(solution)/shard_map/reshape;squeeze | solution.py:11
  192.7 10.9 %reshape_squeeze.26 = bf16[32,32,32,32]{3,2,1,0:T(8,128)(2,1)} reshape(bf16[1,1024,1024]{2,1,0:T(8,128)(2,1)} %get-tuple-element.98) | data formatting | bytes 4194304 | tf_op jit(solution)/shard_map/reshape;squeeze | solution.py:11
  203.6 10.9 %reshape_squeeze.25 = bf16[32,32,32,32]{3,2,1,0:T(8,128)(2,1)} reshape(bf16[1,1024,1024]{2,1,0:T(8,128)(2,1)} %get-tuple-element.99) | data formatting | bytes 4194304 | tf_op jit(solution)/shard_map/reshape;squeeze | solution.py:11
  214.5 7.8 %reshape_squeeze.24 = bf16[32,32,32,32]{3,2,1,0:T(8,128)(2,1)} reshape(bf16[1,1024,1024]{2,1,0:T(8,128)(2,1)S(1)} %get-tuple-element.100) | data formatting | bytes 4194304 | tf_op jit(solution)/shard_map/reshape;squeeze | solution.py:11
  223.9 14.2 %reshape.879 = bf16[128,1,8192]{2,1,0:T(2,128)(2,1)} reshape(bf16[128,2,4096]{2,1,0:T(2,128)(2,1)} %all-to-all-done) | data formatting | bytes 4194304
  269.0 8.9 %fusion.69 = f32[8,32,32]{2,0,1:T(8,128)S(1)} fusion(bf16[32,32,32,32]{3,2,1,0:T(8,128)(2,1)} %reshape_squeeze.31, bf16[8,32,32]{2,1,0:T(8,128)(2,1)S(1)} %squeeze.230, f32[]{:T(128)S(6)} %mul.410), kind=kOutput, calls=%fused_computation.126 | convolution fusion | flops 16785408 | bytes 2146308 | tf_op jit(solution)/shard_map/pqrs,kps->kqr/dot_general | solution.py:18
  309.5 8.9 %fusion.67 = f32[8,32,32]{2,0,1:T(8,128)S(1)} fusion(bf16[32,32,32,32]{3,2,1,0:T(8,128)(2,1)} %reshape_squeeze.30, bf16[8,32,32]{2,1,0:T(8,128)(2,1)S(1)} %squeeze.223, f32[]{:T(128)S(6)} %mul.399), kind=kOutput, calls=%fused_computation.124 | convolution fusion | flops 16785408 | bytes 2146308 | tf_op jit(solution)/shard_map/pqrs,kps->kqr/dot_general | solution.py:18
  350.2 8.9 %fusion.65 = f32[8,32,32]{2,0,1:T(8,128)S(1)} fusion(bf16[32,32,32,32]{3,2,1,0:T(8,128)(2,1)} %reshape_squeeze.29, bf16[8,32,32]{2,1,0:T(8,128)(2,1)S(1)} %squeeze.216, f32[]{:T(128)S(6)} %mul.388), kind=kOutput, calls=%fused_computation.122 | convolution fusion | flops 16785408 | bytes 2146308 | tf_op jit(solution)/shard_map/pqrs,kps->kqr/dot_general | solution.py:18
  390.7 8.9 %fusion.63 = f32[8,32,32]{2,0,1:T(8,128)S(1)} fusion(bf16[32,32,32,32]{3,2,1,0:T(8,128)(2,1)} %reshape_squeeze.28, bf16[8,32,32]{2,1,0:T(8,128)(2,1)S(1)} %squeeze.209, f32[]{:T(128)S(6)} %mul.377), kind=kOutput, calls=%fused_computation.120 | convolution fusion | flops 16785408 | bytes 2146308 | tf_op jit(solution)/shard_map/pqrs,kps->kqr/dot_general | solution.py:18
  406.0 7.8 %fusion.146 = f32[8,32,32]{2,0,1:T(8,128)S(1)} fusion(bf16[32,32,32,32]{3,2,1,0:T(8,128)(2,1)} %reshape_squeeze.27, bf16[8,32,32]{2,1,0:T(8,128)(2,1)S(1)} %squeeze.198, f32[]{:T(128)S(6)} %mul.362), kind=kOutput, calls=%fused_computation.153 | convolution fusion | flops 16785408 | bytes 2146308 | tf_op jit(solution)/shard_map/pqrs,krs->kpq/dot_general | solution.py:14
  431.2 8.9 %fusion.61 = f32[8,32,32]{2,0,1:T(8,128)S(1)} fusion(bf16[32,32,32,32]{3,2,1,0:T(8,128)(2,1)} %reshape_squeeze.27, bf16[8,32,32]{2,1,0:T(8,128)(2,1)S(1)} %squeeze.202, f32[]{:T(128)S(6)} %mul.366), kind=kOutput, calls=%fused_computation.118 | convolution fusion | flops 16785408 | bytes 2146308 | tf_op jit(solution)/shard_map/pqrs,kps->kqr/dot_general | solution.py:18
  472.1 8.9 %fusion.59 = f32[8,32,32]{2,0,1:T(8,128)S(1)} fusion(bf16[32,32,32,32]{3,2,1,0:T(8,128)(2,1)} %reshape_squeeze.26, bf16[8,32,32]{2,1,0:T(8,128)(2,1)S(1)} %squeeze.195, f32[]{:T(128)S(6)} %mul.355), kind=kOutput, calls=%fused_computation.116 | convolution fusion | flops 16785408 | bytes 2146308 | tf_op jit(solution)/shard_map/pqrs,kps->kqr/dot_general | solution.py:18
  513.9 8.9 %fusion.57 = f32[8,32,32]{2,0,1:T(8,128)S(1)} fusion(bf16[32,32,32,32]{3,2,1,0:T(8,128)(2,1)} %reshape_squeeze.25, bf16[8,32,32]{2,1,0:T(8,128)(2,1)S(1)} %squeeze.188, f32[]{:T(128)S(6)} %mul.344), kind=kOutput, calls=%fused_computation.114 | convolution fusion | flops 16785408 | bytes 2146308 | tf_op jit(solution)/shard_map/pqrs,kps->kqr/dot_general | solution.py:18
  535.6 8.9 %fusion.55 = f32[8,32,32]{2,0,1:T(8,128)S(1)} fusion(bf16[32,32,32,32]{3,2,1,0:T(8,128)(2,1)} %reshape_squeeze.24, bf16[8,32,32]{2,1,0:T(8,128)(2,1)S(1)} %squeeze.181, f32[]{:T(128)S(6)} %mul.333), kind=kOutput, calls=%fused_computation.112 | convolution fusion | flops 16785408 | bytes 2146308 | tf_op jit(solution)/shard_map/pqrs,kps->kqr/dot_general | solution.py:18
  616.1 62.0 %all_to_all.21 = f32[128,1,8192]{2,1,0:T(1,128)} all-to-all(f32[128,1,8192]{2,1,0:T(1,128)S(1)} %all_to_all.16), channel_id=1, replica_groups=mesh['row'=8,'col'=16] {'row','col'}, dimensions={0} | all-to-all | bytes 8388608 | tf_op jit(solution)/shard_map/all_to_all | solution.py:82
  678.1 11.7 %scatter_custom_fusion.10 = f32[128,8192]{1,0:T(8,128)} fusion(s32[128]{0:T(128)} %get-tuple-element.132, f32[128,1,8192]{2,1,0:T(1,128)} %all_to_all.21, f32[]{:T(128)} %constant.78.clone.1), kind=kCustom, calls=%fused_computation.52 | custom fusion | flops 1048576 | bytes 8389120 | tf_op jit(solution)/shard_map/scatter-add | solution.py:84
  (303 shorter events, 328.5 us)
Async XLA Ops:
  72.6 21.8 %copy-start.2 = (s32[992]{0:T(1024)S(1)}, s32[992]{0:T(1024)}, u32[]{:S(2)}) copy-start(s32[992]{0:T(1024)} %param.8) | copy-start | bytes 11908
  82.5 141.4 %all-to-all-start = ((bf16[128,2,4096]{2,1,0:T(2,128)(2,1)}), bf16[128,2,4096]{2,1,0:T(2,128)(2,1)}, u32[]{:S(2)}, u32[]{:S(2)}) async-start(bf16[128,2,4096]{2,1,0:T(2,128)(2,1)} %reshape.878), calls=%async_computation | async-start | bytes 4194304 | tf_op jit(solution)/shard_map/all_to_all | solution.py:67
  100.4 27.2 %copy-start.17 = (s32[992]{0:T(1024)S(1)}, s32[992]{0:T(1024)}, u32[]{:S(2)}) copy-start(s32[992]{0:T(1024)} %param.9) | copy-start | bytes 11908
  222.6 0.5 copy-start.3
  222.6 0.6 copy-start.5
  222.7 0.6 copy-start.7
  222.7 0.6 copy-start.9
  222.7 0.5 copy-start.11
  222.7 0.6 copy-start.13
  223.1 28.3 %copy-start.15 = (s32[6]{0:T(128)}, s32[6]{0:T(128)S(1)}, u32[]{:S(2)}) copy-start(s32[6]{0:T(128)S(1)} %get-tuple-element.134) | copy-start | bytes 76
  223.1 28.3 %copy-start.18 = (s32[6]{0:T(128)}, s32[6]{0:T(128)S(1)}, u32[]{:S(2)}) copy-start(s32[6]{0:T(128)S(1)} %get-tuple-element.133) | copy-start | bytes 76
  562.1 11.5 %copy-start = (f32[1,8192]{1,0:T(1,128)S(1)}, f32[1,8192]{1,0:T(1,128)}, u32[]{:S(2)}) copy-start(f32[1,8192]{1,0:T(1,128)} %stack_reshape.154) | copy-start | bytes 98308
  562.1 11.5 %copy-start.1 = (f32[1,8192]{1,0:T(1,128)S(1)}, f32[1,8192]{1,0:T(1,128)}, u32[]{:S(2)}) copy-start(f32[1,8192]{1,0:T(1,128)} %stack_reshape.155) | copy-start | bytes 98308
  562.1 11.8 %copy-start.16 = (s32[6]{0:T(128)S(1)}, s32[6]{0:T(128)}, u32[]{:S(2)}) copy-start(s32[6]{0:T(128)} %copy-done.15) | copy-start | bytes 76
  562.3 16.8 %copy-start.14 = (s32[6]{0:T(128)S(1)}, s32[6]{0:T(128)}, u32[]{:S(2)}) copy-start(s32[6]{0:T(128)} %copy-done.13) | copy-start | bytes 76
  569.9 14.5 %copy-start.12 = (s32[6]{0:T(128)S(1)}, s32[6]{0:T(128)}, u32[]{:S(2)}) copy-start(s32[6]{0:T(128)} %copy-done.11) | copy-start | bytes 76
  573.5 16.1 %copy-start.10 = (s32[6]{0:T(128)S(1)}, s32[6]{0:T(128)}, u32[]{:S(2)}) copy-start(s32[6]{0:T(128)} %copy-done.9) | copy-start | bytes 76
  578.8 16.1 %copy-start.8 = (s32[6]{0:T(128)S(1)}, s32[6]{0:T(128)}, u32[]{:S(2)}) copy-start(s32[6]{0:T(128)} %copy-done.7) | copy-start | bytes 76
  584.1 16.3 %copy-start.6 = (s32[6]{0:T(128)S(1)}, s32[6]{0:T(128)}, u32[]{:S(2)}) copy-start(s32[6]{0:T(128)} %copy-done.5) | copy-start | bytes 76
  589.4 16.3 %copy-start.4 = (s32[6]{0:T(128)S(1)}, s32[6]{0:T(128)}, u32[]{:S(2)}) copy-start(s32[6]{0:T(128)} %copy-done.3) | copy-start | bytes 76
where the time goes:
time: 702 us; the launch traced here: 690 us
  matrix products  302 us (43%)
  local copies, waits for them, and re-layouts  221 us (31%)
  other arithmetic  65.9 us (9%)
  blocking collectives  62 us (9%)
  between operations  26.2 us (4%)
  starting transfers between devices  12 us (2%)
    another operation x8, local copies, waits for them, and re-layouts, quartet_terms(): four = block.reshape(BS, BS, BS, BS)  84.1 us
    dot_general x8, matrix products, quartet_terms(): k_qr = jnp.einsum('pqrs,kps->kqr', four, d_ps, preferred_element_type=f32)  70.9 us
    all_to_all x1, blocking collectives, local(): lax.all_to_all(returned, ('row', 'col'), split_axis=0, concat_axis=0, til...  62 us
    dot_general x8, matrix products, quartet_terms(): j_pq = jnp.einsum('pqrs,krs->kpq', four, d_rs, preferred_element_type=f32)  60.8 us
    dot_general x8, matrix products, quartet_terms(): j_rs = jnp.einsum('pqrs,kpq->krs', four, d_pq, preferred_element_type=f32)  47.2 us
    dot_general x8, matrix products, quartet_terms(): k_pr = jnp.einsum('pqrs,kqs->kpr', four, d_qs, preferred_element_type=f32)  46.8 us
    dot_general x8, matrix products, quartet_terms(): k_ps = jnp.einsum('pqrs,kqr->kps', four, d_qr, preferred_element_type=f32)  38.5 us
    dot_general x8, matrix products, quartet_terms(): k_qs = jnp.einsum('pqrs,kpr->kqs', four, d_pr, preferred_element_type=f32)  38.3 us
  transfers between devices with their start and end apart: 1, of which 0 were waited for; matrix products, arithmetic and copies ran while one was open for 15% of the time, Pallas kernels for 0%

commit v1 on v0

v1 whole, which is shorter than its diff:
```python
import functools

import jax
import jax.numpy as jnp
from jax import lax
from jax.experimental import pallas as pl
from jax.experimental.pallas import tpu as pltpu
from jax.sharding import PartitionSpec as P

BS = 32
PERT = 8
SLOTS = 8
N_ROW = 8
N_COL = 16
DEVS = N_ROW * N_COL
ROWS_LOC = 16
COLS_LOC = 8
BLOCKS = ROWS_LOC * COLS_LOC
PITCH = 72
GPITCH = 40
MESH = pl.DeviceIdType.MESH
F32 = jnp.float32
BF16 = jnp.bfloat16
VMEM = pltpu.VMEM
SMEM = pltpu.SMEM


def here():
    return lax.axis_index("row"), lax.axis_index("col")


def enter_all(col_sem):
    r, c = here()
    first = pltpu.get_barrier_semaphore()

    def greet_row(i, _):
        pl.semaphore_signal(first, inc=1, device_id=((r + i) % N_ROW, c), device_id_type=MESH)
        return 0

    def greet_col(i, _):
        pl.semaphore_signal(first, inc=1, device_id=(r, (c + i) % N_COL), device_id_type=MESH)
        return 0

    def pass_on(i, _):
        pl.semaphore_signal(col_sem, inc=1, device_id=(r, (c + i) % N_COL), device_id_type=MESH)
        return 0

    lax.fori_loop(1, N_ROW, greet_row, 0)
    lax.fori_loop(1, N_COL, greet_col, 0)
    pl.semaphore_wait(first, N_ROW + N_COL - 2)
    lax.fori_loop(1, N_COL, pass_on, 0)
    pl.semaphore_wait(col_sem, N_COL - 1)


def partner(step):
    r, c = here()
    return (r + step // N_COL) % N_ROW, (c + step % N_COL) % N_COL


def exchange(src, dst, send_sem, recv_sem):
    r, c = here()
    me = r * N_COL + c

    def post(step, _):
        tr, tc = partner(step)
        pltpu.make_async_remote_copy(
            src_ref=src.at[tr * N_COL + tc],
            dst_ref=dst.at[me],
            send_sem=send_sem,
            recv_sem=recv_sem,
            device_id=(tr, tc),
            device_id_type=MESH,
        ).start()
        return 0

    lax.fori_loop(1, DEVS, post, 0)
    dst[me] = src[me]
    done = pltpu.make_async_remote_copy(
        src_ref=src.at[pl.ds(0, DEVS - 1)],
        dst_ref=dst.at[pl.ds(0, DEVS - 1)],
        send_sem=send_sem,
        recv_sem=recv_sem,
        device_id=(r, c),
        device_id_type=MESH,
    )
    done.wait_send()
    done.wait_recv()


def fetch_kernel(table, dens, out, blocks, send, send_sem, recv_sem, col_sem):
    flat = blocks.reshape(BLOCKS * PITCH, 128)

    def split(a, _):
        for ck in range(64):
            k, c = ck // 8, ck % 8
            flat[pl.ds(a * 8 * PITCH + c * 8 + k, 8, stride=PITCH), :] = dens[a, :, ck * 128 : (ck + 1) * 128]
        return 0

    lax.fori_loop(0, ROWS_LOC, split, 0)

    def pick(h, _):
        send[h] = blocks[table[h]][:64].astype(BF16)
        return 0

    lax.fori_loop(0, DEVS, pick, 0)
    enter_all(col_sem)
    exchange(send, out, send_sem, recv_sem)


def give_kernel(src, out, send_sem, recv_sem, col_sem):
    enter_all(col_sem)
    exchange(src, out, send_sem, recv_sem)


def group_of(shape):
    return lax.broadcasted_iota(jnp.int32, shape, 1) // 32


def nat_fold(parts):
    g = group_of((8, 128))
    lo = g < 2
    ev = g % 2 == 0
    s = []
    for o in parts:
        s.append(jnp.where(g == 0, o[0:8], jnp.where(g == 1, o[8:16], jnp.where(g == 2, o[16:24], o[24:32]))))
    c02 = jnp.where(lo, s[0], s[2]) + pltpu.roll(jnp.where(lo, s[2], s[0]), 64, 1)
    c13 = jnp.where(lo, s[1], s[3]) + pltpu.roll(jnp.where(lo, s[3], s[1]), 64, 1)
    return jnp.where(ev, c02, c13) + jnp.where(ev, pltpu.roll(c02, 96, 1), pltpu.roll(c13, 32, 1))


def spread(d):
    g = group_of((8, 128))
    rolled = [d] + [pltpu.roll(d, 32 * i, 1) for i in range(1, 4)]
    return [
        jnp.concatenate([jnp.where(g == ul, rolled[(ul - xl) % 4], 0.0) for ul in range(4)], 0) for xl in range(4)
    ]


def stacked(src, q, lead, pitch):
    return jnp.concatenate([src[q, pl.ds(lead * pitch, 32), uh * 128 : (uh + 1) * 128] for uh in range(8)], 0)


def cross(tiles, left, d_nat):
    outs, acc = [], None
    for half in range(2):
        exp = spread(d_nat[:, half * 128 : (half + 1) * 128])
        parts = []
        for pair in range(2):
            w = jnp.concatenate([tiles[half * 4 + pair * 2], tiles[half * 4 + pair * 2 + 1]], 1)
            o = jnp.dot(left, w, preferred_element_type=F32)
            parts += [o[:, :128], o[:, 128:]]
            e = jnp.concatenate([exp[pair * 2], exp[pair * 2 + 1]], 1).astype(BF16)
            t = lax.dot_general(e, w, (((1,), (1,)), ((), ())), preferred_element_type=F32)
            acc = t if acc is None else acc + t
        outs.append(nat_fold(parts))
    return outs, acc


def perm_matrix():
    i = lax.broadcasted_iota(jnp.int32, (1024, 1024), 0)
    j = lax.broadcasted_iota(jnp.int32, (1024, 1024), 1)
    return jnp.where((i % 4) * 256 + ((i // 4) % 8) * 32 + i // 32 == j, 1.0, 0.0).astype(BF16)


def rows_of(x):
    return jnp.concatenate([x[:, c * 128 : (c + 1) * 128] for c in range(8)], 0)


def lanes_of(x):
    return jnp.concatenate([x[c * 8 : (c + 1) * 8, :] for c in range(8)], 1)


def quartet_kernel(owners, factor, back, recv, integ, perm, send, a_buf, g_buf, f_buf, d_nat, d_in, d_perm, o_perm, contrib, sem):
    loads = [pltpu.make_async_copy(integ.at[q], a_buf.at[q % 2], sem.at[q % 2]) for q in range(SLOTS)]
    loads[0].start()

    def collect(i, _):
        d_nat[i] = lanes_of(recv[owners[i]].astype(F32))
        return 0

    lax.fori_loop(0, 48, collect, 0)
    for q in range(SLOTS):
        for n, t in enumerate((4, 2)):
            d_in[pl.ds((q * 2 + n) * 8, 8), :] = d_nat[q * 6 + t]
    moved = jnp.dot(d_in[...].astype(BF16), perm[...], preferred_element_type=F32)
    d_perm[...] = moved.reshape(16, 8, 1024)

    def one(q, _):
        slot = q % 2
        pltpu.make_async_copy(integ.at[q], a_buf.at[slot], sem.at[slot]).wait()

        @pl.when(q + 1 < SLOTS)
        def _():
            pltpu.make_async_copy(integ.at[q + 1], a_buf.at[1 - slot], sem.at[1 - slot]).start()

        def widen(x, _):
            for uh in range(8):
                f_buf[uh, pl.ds(x * GPITCH, 32), :] = a_buf[slot, pl.ds(x * 32, 32), uh * 128 : (uh + 1) * 128].astype(F32)
            return 0

        lax.fori_loop(0, 32, widen, 0)

        def regroup(y, _):
            for uh in range(8):
                g_buf[0, pl.ds(y * 32, 32), uh * 128 : (uh + 1) * 128] = f_buf[uh, pl.ds(y, 32, stride=GPITCH), :].astype(BF16)
            return 0

        lax.fori_loop(0, 32, regroup, 0)
        base = q * 6
        fac = factor[q]
        left_ps = jnp.concatenate([d_perm[q * 2][:, u * 256 : (u + 1) * 256] for u in range(4)], 0).astype(BF16)
        left_qs = jnp.concatenate([d_perm[q * 2 + 1][:, u * 256 : (u + 1) * 256] for u in range(4)], 0).astype(BF16)
        d_rs = d_nat[base + 1].astype(BF16)
        j_rs = jnp.zeros((8, 1024), F32)
        k_qr = jnp.zeros((32, 256), F32)
        k_pr = jnp.zeros((32, 256), F32)
        j_pq, k_ps, k_qs = [], [], []
        for xg in range(4):
            cols = slice(xg * 256, (xg + 1) * 256)
            a_rows = a_buf[slot, xg * 256 : (xg + 1) * 256, :]
            j_rs = j_rs + jnp.dot(d_nat[base, :, cols].astype(BF16), a_rows, preferred_element_type=F32)
            j_pq.append(lax.dot_general(d_rs, a_rows, (((1,), (1,)), ((), ())), preferred_element_type=F32))
            tiles = [stacked(a_buf, slot, xg * 8 + i, 32) for i in range(8)]
            outs, acc = cross(tiles, left_ps, d_nat[base + 3, :, cols])
            k_ps += outs
            k_qr = k_qr + acc
            tiles = [stacked(g_buf, 0, xg * 8 + i, 32) for i in range(8)]
            outs, acc = cross(tiles, left_qs, d_nat[base + 5, :, cols])
            k_qs += outs
            k_pr = k_pr + acc
        coul = 2.0 * fac
        exch = -0.5 * fac
        contrib[base] = rows_of(coul * jnp.concatenate(j_pq, 1)).astype(BF16)
        contrib[base + 1] = rows_of(coul * j_rs).astype(BF16)
        contrib[base + 3] = jnp.concatenate([exch * x for x in k_ps], 0).astype(BF16)
        contrib[base + 5] = jnp.concatenate([exch * x for x in k_qs], 0).astype(BF16)
        o_perm[q * 2] = exch * jnp.concatenate([k_qr[u * 8 : (u + 1) * 8] for u in range(4)], 1)
        o_perm[q * 2 + 1] = exch * jnp.concatenate([k_pr[u * 8 : (u + 1) * 8] for u in range(4)], 1)
        return 0

    lax.fori_loop(0, SLOTS, one, 0)
    back_in = o_perm[...].reshape(128, 1024).astype(BF16)
    natural = lax.dot_general(back_in, perm[...], (((1,), (1,)), ((), ())), preferred_element_type=F32)
    for q in range(SLOTS):
        for n, t in enumerate((4, 2)):
            at = (q * 2 + n) * 8
            contrib[q * 6 + t] = rows_of(natural[at : at + 8]).astype(BF16)

    def place(o, _):
        send[o] = contrib[back[o]]
        return 0

    lax.fori_loop(0, DEVS, place, 0)


def scatter_kernel(table, arrived, out, acc):
    def clear(i, _):
        acc[pl.ds(i * PITCH, PITCH), :] = jnp.zeros((PITCH, 128), F32)
        return 0

    lax.fori_loop(0, BLOCKS + 1, clear, 0)

    def add(h, _):
        at = pl.multiple_of(table[h] * PITCH, 8)
        acc[pl.ds(at, 64), :] += arrived[h].astype(F32)
        return 0

    lax.fori_loop(0, DEVS, add, 0)

    def join(a, _):
        for ck in range(64):
            k, c = ck // 8, ck % 8
            out[a, :, ck * 128 : (ck + 1) * 128] = acc[pl.ds(a * 8 * PITCH + c * 8 + k, 8, stride=PITCH), :]
        return 0

    lax.fori_loop(0, ROWS_LOC, join, 0)


def tables(quartets, holder, degeneracy):
    me = lax.axis_index("row") * N_COL + lax.axis_index("col")
    q = quartets.T
    first = jnp.stack([q[0], q[2], q[0], q[0], q[1], q[1]])
    second = jnp.stack([q[1], q[3], q[2], q[3], q[2], q[3]])
    owner = first // ROWS_LOC * N_COL + second // COLS_LOC
    local = first % ROWS_LOC * COLS_LOC + second % COLS_LOC
    asked = jnp.sum(jnp.where(owner == me, local + 1, 0), 0)
    devs = jnp.arange(DEVS, dtype=jnp.int32)
    lid = jnp.sum(jnp.where(holder[None, :] == devs[:, None], asked[None, :], 0), 1)
    pick = jnp.maximum(lid - 1, 0)
    target = jnp.where(lid > 0, lid - 1, BLOCKS)
    own = holder == me
    order = jnp.arange(holder.shape[0], dtype=jnp.int32)
    rank = jnp.sum(jnp.where(own[None, :] & (order[None, :] < order[:, None]), 1, 0), 1)
    sel = own[None, :] & (rank[None, :] == jnp.arange(SLOTS, dtype=jnp.int32)[:, None])
    owners = jnp.sum(jnp.where(sel[:, None, :], owner[None], 0), 2)
    deg = jnp.sum(jnp.where(sel, degeneracy[None, :], 0), 1)
    live = (deg > 0)[:, None]
    flat = jnp.where(live, owners, -1).reshape(-1)
    ids = jnp.arange(48, dtype=jnp.int32)
    back = jnp.sum(jnp.where(flat[None, :] == devs[:, None], ids[None, :], 0), 1)
    return pick, target, owners.reshape(-1), deg.astype(F32), back


def vspec():
    return pl.BlockSpec(memory_space=VMEM)


def sspec():
    return pl.BlockSpec(memory_space=SMEM)


def params(**kw):
    return pltpu.CompilerParams(vmem_limit_bytes=56 * 2**20, **kw)


def local(density, integrals, quartets, holder, degeneracy):
    pick, target, owners, factor, back = tables(quartets, holder, degeneracy)
    wire = jax.ShapeDtypeStruct((DEVS, 64, 128), BF16)
    sems = [pltpu.SemaphoreType.DMA, pltpu.SemaphoreType.DMA, pltpu.SemaphoreType.REGULAR]
    recv = pl.pallas_call(
        fetch_kernel,
        out_shape=wire,
        in_specs=[sspec(), vspec()],
        out_specs=vspec(),
        scratch_shapes=[VMEM((BLOCKS, PITCH, 128), F32), VMEM((DEVS, 64, 128), BF16)] + sems,
        compiler_params=params(collective_id=0, has_side_effects=True),
        name="fetch",
    )(pick, density)
    send = pl.pallas_call(
        quartet_kernel,
        out_shape=wire,
        in_specs=[sspec(), sspec(), sspec(), vspec(), pl.BlockSpec(memory_space=pl.ANY), vspec()],
        out_specs=vspec(),
        scratch_shapes=[
            VMEM((2, 1024, 1024), BF16),
            VMEM((1, 1024, 1024), BF16),
            VMEM((8, 32 * GPITCH, 128), F32),
            VMEM((48, 8, 1024), F32),
            VMEM((128, 1024), F32),
            VMEM((16, 8, 1024), F32),
            VMEM((16, 8, 1024), F32),
            VMEM((48, 64, 128), BF16),
            pltpu.SemaphoreType.DMA((2,)),
        ],
        compiler_params=params(),
        name="quartets",
    )(owners, factor, back, recv, integrals, perm_matrix())
    arrived = pl.pallas_call(
        give_kernel,
        out_shape=wire,
        in_specs=[vspec()],
        out_specs=vspec(),
        scratch_shapes=sems,
        compiler_params=params(collective_id=1, has_side_effects=True),
        name="give",
    )(send)
    return pl.pallas_call(
        scatter_kernel,
        out_shape=jax.ShapeDtypeStruct(density.shape, F32),
        in_specs=[sspec(), vspec()],
        out_specs=vspec(),
        scratch_shapes=[VMEM(((BLOCKS + 1) * PITCH, 128), F32)],
        compiler_params=params(),
        name="scatter",
    )(target, arrived)


def solution(mesh):
    return jax.shard_map(
        local,
        mesh=mesh,
        in_specs=(P("row", "col", None), P(("row", "col"), None, None), P(), P(), P()),
        out_specs=P("row", "col", None),
        check_vma=False,
    )
```

time: 702 us -> 143 us (0.20); the launches traced: 690 us -> 143 us
  matrix products: 302 us -> 0 us
  local copies, waits for them, and re-layouts: 221 us -> 2.06 us
  Pallas kernels: 0 us -> 132 us
  blocking collectives: 62 us -> 0 us
  other arithmetic: 65.9 us -> 8.8 us
  between operations: 26.2 us -> 0.1 us
  starting transfers between devices: 12 us -> 0 us
    dot_general x48 -> x0, matrix products: 302 us -> none  [the longest x8 70.9 us: quartet_terms(): k_qr = jnp.einsum('pqrs,kps->kqr', four, d_ps, preferred_element_type=f32)]
    pallas_call x0 -> x4, Pallas kernels: none -> 132 us  [the longest x1 43.5 us: local(): pl.pallas_call(fetch_kernel, out_shape=wire, in_specs=[sspec(), vspec()],...]
    another operation x69 -> x1, local copies, waits for them, and re-layouts: 94.7 us -> 0.04 us  [tables(): first = jnp.stack([q[0], q[2], q[0], q[0], q[1], q[1]])]
    all_to_all x1 -> x0, blocking collectives: 62 us -> none  [local(): lax.all_to_all(returned, ('row', 'col'), split_axis=0, concat_axis=0, til...]
    scatter x2 -> x0, local copies, waits for them, and re-layouts: 61.3 us -> none  [the longest x1 32.6 us: local(): jnp.zeros((devices_all,), jnp.bool_).at[dest_dev].set(True, mode='drop')]
    scatter-add x9 -> x0, other arithmetic: 49.8 us -> none  [the longest x8 38.1 us: local(): returned = returned.at[owners_six].add(stacked)]
    unnamed x41 -> x2, local copies, waits for them, and re-layouts: 23.8 us -> 0.01 us
    slice x11 -> x2, local copies, waits for them, and re-layouts: 17.8 us -> 1.69 us  [the longest x1 0.88 us: tables(): second = jnp.stack([q[1], q[3], q[2], q[3], q[2], q[3]])]
  transfers between devices with their start and end apart: 1 -> 0, of which waited for: 0 -> 0; matrix products, arithmetic and copies ran while one was open for 15% -> 0% of each run, Pallas kernels for 0% -> 0%
where the time goes in v1:
time: 143 us
  Pallas kernels  132 us (92%)
  other arithmetic  8.8 us (6%)
  local copies, waits for them, and re-layouts  2.06 us (1%)
    pallas_call x1, Pallas kernels, local(): pl.pallas_call(fetch_kernel, out_shape=wire, in_specs=[sspec(), vspec()],...  43.5 us
    pallas_call x1, Pallas kernels, local(): pl.pallas_call(quartet_kernel, out_shape=wire, in_specs=[sspec(), sspec()...  43.1 us
    pallas_call x1, Pallas kernels, local(): pl.pallas_call(give_kernel, out_shape=wire, in_specs=[vspec()], out_specs...  38.8 us
    pallas_call x1, Pallas kernels, local(): pl.pallas_call(scatter_kernel, out_shape=jax.ShapeDtypeStruct(density.sha...  6.26 us
    convert_element_type x1, other arithmetic, perm_matrix(): jnp.where(i % 4 * 256 + i // 4 % 8 * 32 + i // 32 == j, 1.0, 0.0)  3.98 us

profile of v1, /device:TPU:1, one launch (start us, length us, event | category | flops | bytes accessed | tf_op | source)
XLA Modules:
  0.0 142.6 jit_solution(16127827677708693254)
XLA Ops:
  0.0 0.7 broadcast_compare_fusion.1
  0.7 0.2 select_reduce_fusion
  0.9 0.8 select_reduce_fusion.3
  1.8 0.6 convert_element_type.6.factor
  2.3 0.1 broadcast_in_dim.117
  2.4 0.1 broadcast_in_dim.118
  2.6 0.9 fusion.26
  3.5 0.8 fusion.27
  4.3 0.1 fusion.12
  4.4 0.2 select_reduce_fusion.2
  4.6 1.0 select_reduce_fusion.1
  5.6 0.1 copy.6
  5.7 0.1 reshape.306.owners
  5.8 0.0 copy-start
  5.8 0.6 select_reduce_fusion.4.back
  6.4 0.5 add_maximum_fusion
  6.9 4.0 %select_convert_fusion.perm = bf16[1024,1024]{1,0:T(8,128)(2,1)} fusion(s32[1024]{0:T(1024)S(1)} %get-tuple-element.15, s32[1024]{0:T(1024)S(1)} %get-tuple-element.21, s32[1024]{0:T(1024)S(1)} %get-tuple-element.16, s32[1024]{0:T(1024)S(1)} %get-tuple-element.22, s32[1024]{0:T(1024)S(1)} %get-tuple-element.17, s32[1024]{0:T(1024)S(1)} %get-tuple-element.18, ...), kind=kLoop, calls=%fused_computation.10 | loop fusion | flops 22020096 | bytes 2124800 | tf_op jit(solution)/shard_map/convert_element_type | solution.py:162
  10.9 43.5 %fetch.1.recv = bf16[128,64,128]{2,1,0:T(8,128)(2,1)} custom-call(s32[128]{0:T(128)} %get-tuple-element.13.table, f32[16,8,8192]{2,1,0:T(8,128)} %dens.1), custom_call_target="tpu_custom_call" | custom-call | tf_op jit(solution)/shard_map/fetch/pallas_call | solution.py:320
  54.4 0.0 copy-done
  54.4 43.1 %quartets.1.src = bf16[128,64,128]{2,1,0:T(8,128)(2,1)} custom-call(s32[48]{0:T(128)} %copy-done, f32[8]{0:T(128)} %convert_element_type.6.factor, s32[128]{0:T(128)} %select_reduce_fusion.4.back, bf16[128,64,128]{2,1,0:T(8,128)(2,1)} %fetch.1.recv, bf16[8,1024,1024]{2,1,0:T(8,128)(2,1)} %integ.1, bf16[1024,1024]{1,0:T(8,128)(2,1)} %select_convert_fusion.perm), custom_call_target="tpu_custom_call" | custom-call | tf_op jit(solution)/shard_map/quartets/pallas_call | solution.py:329
  97.5 38.8 %give.1.arrived = bf16[128,64,128]{2,1,0:T(8,128)(2,1)} custom-call(bf16[128,64,128]{2,1,0:T(8,128)(2,1)} %quartets.1.src), custom_call_target="tpu_custom_call" | custom-call | tf_op jit(solution)/shard_map/give/pallas_call | solution.py:348
  136.3 6.3 %scatter.1 = f32[16,8,8192]{2,1,0:T(8,128)} custom-call(s32[128]{0:T(128)} %get-tuple-element.14.table, bf16[128,64,128]{2,1,0:T(8,128)(2,1)} %give.1.arrived), custom_call_target="tpu_custom_call" | custom-call | tf_op jit(solution)/shard_map/scatter/pallas_call | solution.py:357
  (9 shorter events, 0.1 us)
Async XLA Ops:
  5.8 48.6 %copy-start = (s32[48]{0:T(128)}, s32[48]{0:T(128)S(1)}, u32[]{:S(2)}) copy-start(s32[48]{0:T(128)S(1)} %reshape.306.owners) | copy-start | bytes 580

commit v2 on v1

v2 whole, which is shorter than its diff:
```python
import jax
import jax.numpy as jnp
from jax import lax
from jax.experimental import pallas as pl
from jax.experimental.pallas import tpu as pltpu
from jax.sharding import PartitionSpec as P

BS = 32
PERT = 8
SLOTS = 8
N_ROW = 8
N_COL = 16
DEVS = N_ROW * N_COL
ROWS_LOC = 16
COLS_LOC = 8
BLOCKS = ROWS_LOC * COLS_LOC
PITCH = 72
GPITCH = 40
MESH = pl.DeviceIdType.MESH
F32 = jnp.float32
BF16 = jnp.bfloat16
VMEM = pltpu.VMEM
SMEM = pltpu.SMEM


def here():
    return lax.axis_index("row"), lax.axis_index("col")


def greet():
    r, c = here()
    first = pltpu.get_barrier_semaphore()

    def greet_row(i, _):
        pl.semaphore_signal(first, inc=1, device_id=((r + i) % N_ROW, c), device_id_type=MESH)
        return 0

    def greet_col(i, _):
        pl.semaphore_signal(first, inc=1, device_id=(r, (c + i) % N_COL), device_id_type=MESH)
        return 0

    lax.fori_loop(1, N_ROW, greet_row, 0)
    lax.fori_loop(1, N_COL, greet_col, 0)


def greeted(col_sem):
    r, c = here()

    def pass_on(i, _):
        pl.semaphore_signal(col_sem, inc=1, device_id=(r, (c + i) % N_COL), device_id_type=MESH)
        return 0

    pl.semaphore_wait(pltpu.get_barrier_semaphore(), N_ROW + N_COL - 2)
    lax.fori_loop(1, N_COL, pass_on, 0)


def all_in(col_sem):
    pl.semaphore_wait(col_sem, N_COL - 1)


def partner(step):
    r, c = here()
    return (r + step // N_COL) % N_ROW, (c + step % N_COL) % N_COL


def all_of(src, dst, send_sem, recv_sem):
    return pltpu.make_async_remote_copy(
        src_ref=src.at[pl.ds(0, DEVS - 1)],
        dst_ref=dst.at[pl.ds(0, DEVS - 1)],
        send_sem=send_sem,
        recv_sem=recv_sem,
        device_id=here(),
        device_id_type=MESH,
    )


def post_all(src, dst, send_sem, recv_sem):
    r, c = here()
    me = r * N_COL + c

    def post(step, _):
        tr, tc = partner(step)
        pltpu.make_async_remote_copy(
            src_ref=src.at[tr * N_COL + tc],
            dst_ref=dst.at[me],
            send_sem=send_sem,
            recv_sem=recv_sem,
            device_id=(tr, tc),
            device_id_type=MESH,
        ).start()
        return 0

    lax.fori_loop(1, DEVS, post, 0)
    dst[me] = src[me]


def group_of(shape):
    return lax.broadcasted_iota(jnp.int32, shape, 1) // 32


def nat_fold(parts):
    g = group_of((8, 128))
    lo = g < 2
    ev = g % 2 == 0
    s = []
    for o in parts:
        s.append(jnp.where(g == 0, o[0:8], jnp.where(g == 1, o[8:16], jnp.where(g == 2, o[16:24], o[24:32]))))
    c02 = jnp.where(lo, s[0], s[2]) + pltpu.roll(jnp.where(lo, s[2], s[0]), 64, 1)
    c13 = jnp.where(lo, s[1], s[3]) + pltpu.roll(jnp.where(lo, s[3], s[1]), 64, 1)
    return jnp.where(ev, c02, c13) + jnp.where(ev, pltpu.roll(c02, 96, 1), pltpu.roll(c13, 32, 1))


def spread(d):
    g = group_of((8, 128))
    rolled = [d] + [pltpu.roll(d, 32 * i, 1) for i in range(1, 4)]
    return [
        jnp.concatenate([jnp.where(g == ul, rolled[(ul - xl) % 4], 0.0) for ul in range(4)], 0) for xl in range(4)
    ]


def half_tile(src, q, lead, hf):
    return jnp.concatenate(
        [src[q, pl.ds(pl.multiple_of(lead * 32 + hf * 16, 16), 16), uh * 128 : (uh + 1) * 128] for uh in range(8)], 0
    )


def full_tile(src, q, lead):
    return jnp.concatenate([half_tile(src, q, lead, hf) for hf in range(2)], 0)


def fold_quarter(src, q, left, qt):
    outs = []
    for grp in range(2):
        parts = []
        for pair in range(2):
            lead = qt * 8 + grp * 4 + pair * 2
            w = jnp.concatenate([full_tile(src, q, lead), full_tile(src, q, lead + 1)], 1)
            o = jnp.dot(left, w, preferred_element_type=F32)
            parts += [o[:, :128], o[:, 128:]]
        outs.append(nat_fold(parts))
    return jnp.concatenate(outs, 0)


def spread_half(src, q, d, hf):
    acc = jnp.zeros((32, 128), F32)
    for grp in range(8):
        exp = spread(d[:, grp * 128 : (grp + 1) * 128])
        for pair in range(2):
            lead = grp * 4 + pair * 2
            w = jnp.concatenate([half_tile(src, q, lead, hf), half_tile(src, q, lead + 1, hf)], 1)
            e = jnp.concatenate([exp[pair * 2], exp[pair * 2 + 1]], 1).astype(BF16)
            acc = acc + lax.dot_general(e, w, (((1,), (1,)), ((), ())), preferred_element_type=F32)
    return jnp.concatenate([acc[u * 8 : (u + 1) * 8] for u in range(4)], 1)


def half_perm():
    i = lax.broadcasted_iota(jnp.int32, (512, 512), 0)
    j = lax.broadcasted_iota(jnp.int32, (512, 512), 1)
    return jnp.where((i % 4) * 128 + ((i // 4) % 8) * 16 + i // 32 == j, 1.0, 0.0).astype(BF16)


def two_rows(x):
    return jnp.concatenate([x[:, :128], x[:, 128:]], 0)


def lanes_of(x):
    return jnp.concatenate([x[c * 8 : (c + 1) * 8, :] for c in range(8)], 1)


def fused_kernel(
    pick, owners, factor, back, dens_hbm, integ, out,
    dens, a_all, g_all, work, send, recv, give, d_nat, d_in, left, o_perm, perm, contrib,
    dens_sem, a_sem, send_sem, recv_sem, give_sem, back_sem, col_sem,
):
    r, c = here()
    me = r * N_COL + c
    dens_in = [pltpu.make_async_copy(dens_hbm.at[pl.ds(i * 4, 4)], dens.at[pl.ds(i * 4, 4)], dens_sem.at[i]) for i in range(4)]
    for copy in dens_in:
        copy.start()

    def load(q):
        return pltpu.make_async_copy(integ.at[q], a_all.at[q], a_sem.at[q])

    greet()
    flat = work.reshape(160 * 64, 128)
    for i in range(4):
        dens_in[i].wait()

        def split(a, _):
            for ck in range(64):
                k, cc = ck // 8, ck % 8
                flat[pl.ds(a * 8 * PITCH + cc * 8 + k, 8, stride=PITCH), :] = dens[a, :, ck * 128 : (ck + 1) * 128]
            return 0

        lax.fori_loop(i * 4, i * 4 + 4, split, 0)
    greeted(col_sem)
    for q in range(SLOTS):
        load(q).start()
    blocks = work.at[pl.ds(0, 144)].reshape(BLOCKS, PITCH, 128)

    def choose(h, _):
        send[h] = blocks[pick[h]][:64].astype(BF16)
        return 0

    lax.fori_loop(0, DEVS, choose, 0)
    all_in(col_sem)
    post_all(send, recv, send_sem, recv_sem)
    perm[...] = half_perm()
    wide = work.reshape(8, 32 * GPITCH, 128)

    def regroup(q, _):
        load(q).wait()

        def widen(x, _):
            for uh in range(8):
                wide[uh, pl.ds(x * GPITCH, 32), :] = a_all[q, pl.ds(x * 32, 32), uh * 128 : (uh + 1) * 128].astype(F32)
            return 0

        lax.fori_loop(0, 32, widen, 0)

        def gather(y, _):
            for uh in range(8):
                g_all[q, pl.ds(y * 32, 32), uh * 128 : (uh + 1) * 128] = wide[uh, pl.ds(y, 32, stride=GPITCH), :].astype(BF16)
            return 0

        lax.fori_loop(0, 32, gather, 0)
        return 0

    lax.fori_loop(0, SLOTS, regroup, 0)
    all_of(send, recv, send_sem, recv_sem).wait_recv()

    def collect(i, _):
        d_nat[i] = lanes_of(recv[owners[i]].astype(F32))
        return 0

    lax.fori_loop(0, 48, collect, 0)
    for q in range(SLOTS):
        for n, t in enumerate((4, 2)):
            d_in[pl.ds((q * 2 + n) * 8, 8), :] = d_nat[q * 6 + t]
    for hf in range(2):
        moved = jnp.dot(d_in[:, hf * 512 : (hf + 1) * 512].astype(BF16), perm[...], preferred_element_type=F32)
        for i in range(16):
            rows = moved[i * 8 : (i + 1) * 8]
            left[i, :, hf * 128 : (hf + 1) * 128] = jnp.concatenate(
                [rows[:, u * 128 : (u + 1) * 128] for u in range(4)], 0
            ).astype(BF16)

    def quarter(qt, hf, first):
        span = pl.ds(pl.multiple_of(qt * 256, 256), 256)

        def one(q, _):
            base = q * 6
            coul = 2.0 * factor[q]
            exch = -0.5 * factor[q]
            j_pq = lax.dot_general(
                d_nat[base + 1].astype(BF16), a_all[q, span, :], (((1,), (1,)), ((), ())), preferred_element_type=F32
            )
            contrib[qt, base] = two_rows(coul * j_pq).astype(BF16)
            j_rs = jnp.dot(d_nat[base].astype(BF16), a_all[q, :, span], preferred_element_type=F32)
            contrib[qt, base + 1] = two_rows(coul * j_rs).astype(BF16)
            contrib[qt, base + 3] = (exch * fold_quarter(a_all, q, left[q * 2], qt)).astype(BF16)
            contrib[qt, base + 5] = (exch * fold_quarter(g_all, q, left[q * 2 + 1], qt)).astype(BF16)
            if first:
                o_perm[q * 2] = exch * spread_half(a_all, q, d_nat[base + 3], hf)
                o_perm[q * 2 + 1] = exch * spread_half(g_all, q, d_nat[base + 5], hf)
            return 0

        lax.fori_loop(0, SLOTS, one, 0)
        if first:
            natural = lax.dot_general(
                o_perm[...].reshape(128, 512).astype(BF16), perm[...], (((1,), (1,)), ((), ())), preferred_element_type=F32
            )
            for i in range(16):
                at = (i // 2) * 6 + (4, 2)[i % 2]
                rows = natural[i * 8 : (i + 1) * 8]
                contrib[qt, at] = two_rows(rows[:, :256]).astype(BF16)
                contrib[qt + 1, at] = two_rows(rows[:, 256:]).astype(BF16)

        def place(o, _):
            give[qt, o] = contrib[qt, back[o]]
            return 0

        lax.fori_loop(0, DEVS, place, 0)
        post_all(give.at[qt], out.at[qt], give_sem.at[qt], back_sem.at[qt])

    def half(hf, _):
        quarter(hf * 2, hf, True)
        quarter(hf * 2 + 1, hf, False)
        return 0

    lax.fori_loop(0, 2, half, 0)
    all_of(send, recv, send_sem, recv_sem).wait_send()
    for qt in range(4):
        done = all_of(give.at[qt], out.at[qt], give_sem.at[qt], back_sem.at[qt])
        done.wait_recv()
        done.wait_send()


def scatter_kernel(table, arrived, out, acc):
    def clear(i, _):
        acc[pl.ds(i * PITCH, PITCH), :] = jnp.zeros((PITCH, 128), F32)
        return 0

    lax.fori_loop(0, BLOCKS + 1, clear, 0)

    def add(h, _):
        at = pl.multiple_of(table[h] * PITCH, 8)
        for qt in range(4):
            acc[pl.ds(at + qt * 16, 16), :] += arrived[qt, h].astype(F32)
        return 0

    lax.fori_loop(0, DEVS, add, 0)

    def join(a, _):
        for ck in range(64):
            k, c = ck // 8, ck % 8
            out[a, :, ck * 128 : (ck + 1) * 128] = acc[pl.ds(a * 8 * PITCH + c * 8 + k, 8, stride=PITCH), :]
        return 0

    lax.fori_loop(0, ROWS_LOC, join, 0)


def tables(quartets, holder, degeneracy):
    me = lax.axis_index("row") * N_COL + lax.axis_index("col")
    q = quartets.T
    first = jnp.stack([q[0], q[2], q[0], q[0], q[1], q[1]])
    second = jnp.stack([q[1], q[3], q[2], q[3], q[2], q[3]])
    owner = first // ROWS_LOC * N_COL + second // COLS_LOC
    local = first % ROWS_LOC * COLS_LOC + second % COLS_LOC
    asked = jnp.sum(jnp.where(owner == me, local + 1, 0), 0)
    devs = jnp.arange(DEVS, dtype=jnp.int32)
    lid = jnp.sum(jnp.where(holder[None, :] == devs[:, None], asked[None, :], 0), 1)
    pick = jnp.maximum(lid - 1, 0)
    target = jnp.where(lid > 0, lid - 1, BLOCKS)
    own = holder == me
    order = jnp.arange(holder.shape[0], dtype=jnp.int32)
    rank = jnp.sum(jnp.where(own[None, :] & (order[None, :] < order[:, None]), 1, 0), 1)
    sel = own[None, :] & (rank[None, :] == jnp.arange(SLOTS, dtype=jnp.int32)[:, None])
    owners = jnp.sum(jnp.where(sel[:, None, :], owner[None], 0), 2)
    deg = jnp.sum(jnp.where(sel, degeneracy[None, :], 0), 1)
    live = (deg > 0)[:, None]
    flat = jnp.where(live, owners, -1).reshape(-1)
    ids = jnp.arange(48, dtype=jnp.int32)
    back = jnp.sum(jnp.where(flat[None, :] == devs[:, None], ids[None, :], 0), 1)
    return pick, target, owners.reshape(-1), deg.astype(F32), back


def vspec():
    return pl.BlockSpec(memory_space=VMEM)


def sspec():
    return pl.BlockSpec(memory_space=SMEM)


def params(**kw):
    return pltpu.CompilerParams(vmem_limit_bytes=60 * 2**20, **kw)


def local(density, integrals, quartets, holder, degeneracy):
    pick, target, owners, factor, back = tables(quartets, holder, degeneracy)
    anyspec = pl.BlockSpec(memory_space=pl.ANY)
    dma = pltpu.SemaphoreType.DMA
    arrived = pl.pallas_call(
        fused_kernel,
        out_shape=jax.ShapeDtypeStruct((4, DEVS, 16, 128), BF16),
        in_specs=[sspec(), sspec(), sspec(), sspec(), anyspec, anyspec],
        out_specs=vspec(),
        scratch_shapes=[
            VMEM((ROWS_LOC, COLS_LOC, 8192), F32),
            VMEM((SLOTS, 1024, 1024), BF16),
            VMEM((SLOTS, 1024, 1024), BF16),
            VMEM((160, 64, 128), F32),
            VMEM((DEVS, 64, 128), BF16),
            VMEM((DEVS, 64, 128), BF16),
            VMEM((4, DEVS, 16, 128), BF16),
            VMEM((48, 8, 1024), F32),
            VMEM((128, 1024), F32),
            VMEM((16, 32, 256), BF16),
            VMEM((16, 8, 512), F32),
            VMEM((512, 512), BF16),
            VMEM((4, 48, 16, 128), BF16),
            dma((4,)),
            dma((SLOTS,)),
            dma,
            dma,
            dma((4,)),
            dma((4,)),
            pltpu.SemaphoreType.REGULAR,
        ],
        compiler_params=params(collective_id=0, has_side_effects=True),
        name="fused",
    )(pick, owners, factor, back, density, integrals)
    return pl.pallas_call(
        scatter_kernel,
        out_shape=jax.ShapeDtypeStruct(density.shape, F32),
        in_specs=[sspec(), vspec()],
        out_specs=vspec(),
        scratch_shapes=[VMEM(((BLOCKS + 1) * PITCH, 128), F32)],
        compiler_params=params(),
        name="scatter",
    )(target, arrived)


def solution(mesh):
    return jax.shard_map(
        local,
        mesh=mesh,
        in_specs=(P("row", "col", None), P(("row", "col"), None, None), P(), P(), P()),
        out_specs=P("row", "col", None),
        check_vma=False,
    )
```

time: 143 us -> 105 us (0.73)
  Pallas kernels: 132 us -> 98.2 us
  other arithmetic: 8.8 us -> 4.68 us
    pallas_call x3 -> x1, Pallas kernels: 125 us -> 91.9 us  [local(): pl.pallas_call(fused_kernel, out_shape=jax.ShapeDtypeStruct((4, DEVS, 16,...]
    convert_element_type x1 -> x0, other arithmetic: 3.98 us -> none  [perm_matrix(): jnp.where(i % 4 * 256 + i // 4 % 8 * 32 + i // 32 == j, 1.0, 0.0)]
where the time goes in v2:
time: 105 us
  Pallas kernels  98.2 us (94%)
  other arithmetic  4.68 us (4%)
  local copies, waits for them, and re-layouts  2.06 us (2%)
    pallas_call x1, Pallas kernels, local(): pl.pallas_call(fused_kernel, out_shape=jax.ShapeDtypeStruct((4, DEVS, 16,...  91.9 us
    pallas_call x1, Pallas kernels, local(): pl.pallas_call(scatter_kernel, out_shape=jax.ShapeDtypeStruct(density.sha...  6.32 us

profile of v2, /device:TPU:1, one launch (start us, length us, event | category | flops | bytes accessed | tf_op | source)
XLA Modules:
  0.0 105.0 jit_solution(77210757328476949)
XLA Ops:
  0.0 0.7 broadcast_compare_fusion.1
  0.7 0.2 select_reduce_fusion
  0.9 0.8 select_reduce_fusion.3
  1.7 0.5 convert_element_type.3.factor
  2.3 0.1 broadcast_in_dim.109
  2.3 0.1 broadcast_in_dim.110
  2.4 0.9 fusion.13
  3.3 0.8 fusion.14
  4.2 0.1 fusion.7
  4.3 0.2 select_reduce_fusion.2
  4.5 1.0 select_reduce_fusion.1
  5.5 0.1 copy.6
  5.6 0.1 reshape.306.owners
  5.7 0.0 copy-start
  5.7 0.6 select_reduce_fusion.4.back
  6.3 0.5 add_maximum_fusion
  6.8 0.0 copy-done
  6.8 91.9 %fused.1.arrived = bf16[4,128,16,128]{3,2,1,0:T(8,128)(2,1)} custom-call(s32[128]{0:T(128)} %get-tuple-element.13.pick, s32[48]{0:T(128)} %copy-done, f32[8]{0:T(128)} %convert_element_type.3.factor, s32[128]{0:T(128)} %select_reduce_fusion.4.back, f32[16,8,8192]{2,1,0:T(8,128)} %dens_hbm.1, bf16[8,1024,1024]{2,1,0:T(8,128)(2,1)} %integ.1), custom_call_target="tpu_custom_call" | custom-call | tf_op jit(solution)/shard_map/fused/pallas_call | solution.py:364
  98.7 6.3 %scatter.1 = f32[16,8,8192]{2,1,0:T(8,128)} custom-call(s32[128]{0:T(128)} %get-tuple-element.14.table, bf16[4,128,16,128]{3,2,1,0:T(8,128)(2,1)} %fused.1.arrived), custom_call_target="tpu_custom_call" | custom-call | tf_op jit(solution)/shard_map/scatter/pallas_call | solution.py:394
  (4 shorter events, 0.1 us)
Async XLA Ops:
  5.7 1.1 %copy-start = (s32[48]{0:T(128)}, s32[48]{0:T(128)S(1)}, u32[]{:S(2)}) copy-start(s32[48]{0:T(128)S(1)} %reshape.306.owners) | copy-start | bytes 580

commit v3 on v2

--- a/solution.py
+++ b/solution.py
@@ -58,11 +58,6 @@
     pl.semaphore_wait(col_sem, N_COL - 1)
 
 
-def partner(step):
-    r, c = here()
-    return (r + step // N_COL) % N_ROW, (c + step % N_COL) % N_COL
-
-
 def all_of(src, dst, send_sem, recv_sem):
     return pltpu.make_async_remote_copy(
         src_ref=src.at[pl.ds(0, DEVS - 1)],
@@ -74,23 +69,38 @@
     )
 
 
+def post(src, dst, send_sem, recv_sem, tr, tc):
+    r, c = here()
+    pltpu.make_async_remote_copy(
+        src_ref=src.at[tr * N_COL + tc],
+        dst_ref=dst.at[r * N_COL + c],
+        send_sem=send_sem,
+        recv_sem=recv_sem,
+        device_id=(tr, tc),
+        device_id_type=MESH,
+    ).start()
+
+
+def post_row(src, dst, send_sem, recv_sem, i):
+    r, c = here()
+    tr = lax.rem(r + i, N_ROW)
+    for j in range(1, N_COL):
+        post(src, dst, send_sem, recv_sem, tr, lax.rem(c + j, N_COL))
+
+    @pl.when(i < N_ROW - 1)
+    def _():
+        post(src, dst, send_sem, recv_sem, lax.rem(r + i + 1, N_ROW), c)
+
+
 def post_all(src, dst, send_sem, recv_sem):
     r, c = here()
     me = r * N_COL + c
 
-    def post(step, _):
-        tr, tc = partner(step)
-        pltpu.make_async_remote_copy(
-            src_ref=src.at[tr * N_COL + tc],
-            dst_ref=dst.at[me],
-            send_sem=send_sem,
-            recv_sem=recv_sem,
-            device_id=(tr, tc),
-            device_id_type=MESH,
-        ).start()
-        return 0
-
-    lax.fori_loop(1, DEVS, post, 0)
+    def row(i, _):
+        post_row(src, dst, send_sem, recv_sem, i)
+        return 0
+
+    lax.fori_loop(0, N_ROW, row, 0)
     dst[me] = src[me]
 
 
@@ -124,29 +134,25 @@
     )
 
 
-def full_tile(src, q, lead):
-    return jnp.concatenate([half_tile(src, q, lead, hf) for hf in range(2)], 0)
-
-
-def fold_quarter(src, q, left, qt):
+def fold_quarter(src, q, left, qt, kh):
     outs = []
     for grp in range(2):
         parts = []
         for pair in range(2):
             lead = qt * 8 + grp * 4 + pair * 2
-            w = jnp.concatenate([full_tile(src, q, lead), full_tile(src, q, lead + 1)], 1)
+            w = jnp.concatenate([half_tile(src, q, lead, kh), half_tile(src, q, lead + 1, kh)], 1)
             o = jnp.dot(left, w, preferred_element_type=F32)
             parts += [o[:, :128], o[:, 128:]]
         outs.append(nat_fold(parts))
     return jnp.concatenate(outs, 0)
 
 
-def spread_half(src, q, d, hf):
+def spread_half(src, q, d, hf, kh):
     acc = jnp.zeros((32, 128), F32)
-    for grp in range(8):
+    for grp in range(4):
         exp = spread(d[:, grp * 128 : (grp + 1) * 128])
         for pair in range(2):
-            lead = grp * 4 + pair * 2
+            lead = kh * 16 + grp * 4 + pair * 2
             w = jnp.concatenate([half_tile(src, q, lead, hf), half_tile(src, q, lead + 1, hf)], 1)
             e = jnp.concatenate([exp[pair * 2], exp[pair * 2 + 1]], 1).astype(BF16)
             acc = acc + lax.dot_general(e, w, (((1,), (1,)), ((), ())), preferred_element_type=F32)
@@ -164,16 +170,15 @@
 
 
 def lanes_of(x):
-    return jnp.concatenate([x[c * 8 : (c + 1) * 8, :] for c in range(8)], 1)
+    return jnp.concatenate([x[c * 8 : (c + 1) * 8, :] for c in range(x.shape[0] // 8)], 1)
 
 
 def fused_kernel(
     pick, owners, factor, back, dens_hbm, integ, out,
-    dens, a_all, g_all, work, send, recv, give, d_nat, d_in, left, o_perm, perm, contrib,
+    dens, a_all, g_all, work, send, recv0, recv1, give, d_nat, d_in, left, acc, o_acc, o_perm, perm, contrib,
     dens_sem, a_sem, send_sem, recv_sem, give_sem, back_sem, col_sem,
 ):
-    r, c = here()
-    me = r * N_COL + c
+    recv = (recv0, recv1)
     dens_in = [pltpu.make_async_copy(dens_hbm.at[pl.ds(i * 4, 4)], dens.at[pl.ds(i * 4, 4)], dens_sem.at[i]) for i in range(4)]
     for copy in dens_in:
         copy.start()
@@ -199,12 +204,15 @@
     blocks = work.at[pl.ds(0, 144)].reshape(BLOCKS, PITCH, 128)
 
     def choose(h, _):
-        send[h] = blocks[pick[h]][:64].astype(BF16)
+        block = blocks[pick[h]].astype(BF16)
+        send[0, h] = block[:32]
+        send[1, h] = block[32:64]
         return 0
 
     lax.fori_loop(0, DEVS, choose, 0)
     all_in(col_sem)
-    post_all(send, recv, send_sem, recv_sem)
+    for kh in range(2):
+        post_all(send.at[kh], recv[kh], send_sem.at[kh], recv_sem.at[kh])
     perm[...] = half_perm()
     wide = work.reshape(8, 32 * GPITCH, 128)
 
@@ -227,42 +235,68 @@
         return 0
 
     lax.fori_loop(0, SLOTS, regroup, 0)
-    all_of(send, recv, send_sem, recv_sem).wait_recv()
-
-    def collect(i, _):
-        d_nat[i] = lanes_of(recv[owners[i]].astype(F32))
-        return 0
-
-    lax.fori_loop(0, 48, collect, 0)
-    for q in range(SLOTS):
-        for n, t in enumerate((4, 2)):
-            d_in[pl.ds((q * 2 + n) * 8, 8), :] = d_nat[q * 6 + t]
-    for hf in range(2):
-        moved = jnp.dot(d_in[:, hf * 512 : (hf + 1) * 512].astype(BF16), perm[...], preferred_element_type=F32)
+    def take_half(kh):
+        all_of(send.at[kh], recv[kh], send_sem.at[kh], recv_sem.at[kh]).wait_recv()
+
+        def collect(q, _):
+            for t in range(6):
+                d_nat[kh, q * 6 + t] = lanes_of(recv[kh][owners[q * 6 + t]].astype(F32))
+            for n, t in enumerate((4, 2)):
+                d_in[pl.ds(pl.multiple_of((q * 2 + n) * 8, 8), 8), :] = d_nat[kh, q * 6 + t]
+            return 0
+
+        lax.fori_loop(0, SLOTS, collect, 0)
+        moved = jnp.dot(d_in[...].astype(BF16), perm[...], preferred_element_type=F32)
         for i in range(16):
             rows = moved[i * 8 : (i + 1) * 8]
-            left[i, :, hf * 128 : (hf + 1) * 128] = jnp.concatenate(
-                [rows[:, u * 128 : (u + 1) * 128] for u in range(4)], 0
-            ).astype(BF16)
+            left[kh, i] = jnp.concatenate([rows[:, u * 128 : (u + 1) * 128] for u in range(4)], 0).astype(BF16)
+
+    def coulomb(kh, q, qt):
+        span = pl.ds(pl.multiple_of(qt * 256, 256), 256)
+        base = q * 6
+        j_pq = lax.dot_general(
+            d_nat[kh, base + 1].astype(BF16),
+            a_all[q, span, kh * 512 : (kh + 1) * 512],
+            (((1,), (1,)), ((), ())),
+            preferred_element_type=F32,
+        )
+        j_rs = jnp.dot(
+            d_nat[kh, base].astype(BF16), a_all[q, kh * 512 : (kh + 1) * 512, span], preferred_element_type=F32
+        )
+        return two_rows(j_pq), two_rows(j_rs)
+
+    def first_part(q, _):
+        base = q * 6
+        for qt in range(4):
+            acc[qt, base], acc[qt, base + 1] = coulomb(0, q, qt)
+            acc[qt, base + 3] = fold_quarter(a_all, q, left[0, q * 2], qt, 0)
+            acc[qt, base + 5] = fold_quarter(g_all, q, left[0, q * 2 + 1], qt, 0)
+        for hf in range(2):
+            o_acc[hf, q * 2] = spread_half(a_all, q, d_nat[0, base + 3], hf, 0)
+            o_acc[hf, q * 2 + 1] = spread_half(g_all, q, d_nat[0, base + 5], hf, 0)
+        return 0
+
+    take_half(0)
+    lax.fori_loop(0, SLOTS, first_part, 0)
+    take_half(1)
 
     def quarter(qt, hf, first):
-        span = pl.ds(pl.multiple_of(qt * 256, 256), 256)
-
         def one(q, _):
             base = q * 6
             coul = 2.0 * factor[q]
             exch = -0.5 * factor[q]
-            j_pq = lax.dot_general(
-                d_nat[base + 1].astype(BF16), a_all[q, span, :], (((1,), (1,)), ((), ())), preferred_element_type=F32
-            )
-            contrib[qt, base] = two_rows(coul * j_pq).astype(BF16)
-            j_rs = jnp.dot(d_nat[base].astype(BF16), a_all[q, :, span], preferred_element_type=F32)
-            contrib[qt, base + 1] = two_rows(coul * j_rs).astype(BF16)
-            contrib[qt, base + 3] = (exch * fold_quarter(a_all, q, left[q * 2], qt)).astype(BF16)
-            contrib[qt, base + 5] = (exch * fold_quarter(g_all, q, left[q * 2 + 1], qt)).astype(BF16)
+            j_pq, j_rs = coulomb(1, q, qt)
+            contrib[qt, base] = (coul * (acc[qt, base] + j_pq)).astype(BF16)
+            contrib[qt, base + 1] = (coul * (acc[qt, base + 1] + j_rs)).astype(BF16)
+            k_ps = acc[qt, base + 3] + fold_quarter(a_all, q, left[1, q * 2], qt, 1)
+            contrib[qt, base + 3] = (exch * k_ps).astype(BF16)
+            k_qs = acc[qt, base + 5] + fold_quarter(g_all, q, left[1, q * 2 + 1], qt, 1)
+            contrib[qt, base + 5] = (exch * k_qs).astype(BF16)
             if first:
-                o_perm[q * 2] = exch * spread_half(a_all, q, d_nat[base + 3], hf)
-                o_perm[q * 2 + 1] = exch * spread_half(g_all, q, d_nat[base + 5], hf)
+                k_qr = o_acc[hf, q * 2] + spread_half(a_all, q, d_nat[1, base + 3], hf, 1)
+                o_perm[q * 2] = exch * k_qr
+                k_pr = o_acc[hf, q * 2 + 1] + spread_half(g_all, q, d_nat[1, base + 5], hf, 1)
+                o_perm[q * 2 + 1] = exch * k_pr
             return 0
 
         lax.fori_loop(0, SLOTS, one, 0)
@@ -276,11 +310,12 @@
                 contrib[qt, at] = two_rows(rows[:, :256]).astype(BF16)
                 contrib[qt + 1, at] = two_rows(rows[:, 256:]).astype(BF16)
 
-        def place(o, _):
-            give[qt, o] = contrib[qt, back[o]]
-            return 0
-
-        lax.fori_loop(0, DEVS, place, 0)
+        def place(i, _):
+            for j in range(8):
+                give[qt, i * 8 + j] = contrib[qt, back[i * 8 + j]]
+            return 0
+
+        lax.fori_loop(0, DEVS // 8, place, 0)
         post_all(give.at[qt], out.at[qt], give_sem.at[qt], back_sem.at[qt])
 
     def half(hf, _):
@@ -289,7 +324,8 @@
         return 0
 
     lax.fori_loop(0, 2, half, 0)
-    all_of(send, recv, send_sem, recv_sem).wait_send()
+    for kh in range(2):
+        all_of(send.at[kh], recv[kh], send_sem.at[kh], recv_sem.at[kh]).wait_send()
     for qt in range(4):
         done = all_of(give.at[qt], out.at[qt], give_sem.at[qt], back_sem.at[qt])
         done.wait_recv()
@@ -371,19 +407,22 @@
             VMEM((SLOTS, 1024, 1024), BF16),
             VMEM((SLOTS, 1024, 1024), BF16),
             VMEM((160, 64, 128), F32),
-            VMEM((DEVS, 64, 128), BF16),
-            VMEM((DEVS, 64, 128), BF16),
+            VMEM((2, DEVS, 32, 128), BF16),
+            VMEM((DEVS, 32, 128), BF16),
+            VMEM((DEVS, 32, 128), BF16),
             VMEM((4, DEVS, 16, 128), BF16),
-            VMEM((48, 8, 1024), F32),
-            VMEM((128, 1024), F32),
-            VMEM((16, 32, 256), BF16),
+            VMEM((2, 48, 8, 512), F32),
+            VMEM((128, 512), F32),
+            VMEM((2, 16, 32, 128), BF16),
+            VMEM((4, 48, 16, 128), F32),
+            VMEM((2, 16, 8, 512), F32),
             VMEM((16, 8, 512), F32),
             VMEM((512, 512), BF16),
             VMEM((4, 48, 16, 128), BF16),
             dma((4,)),
             dma((SLOTS,)),
-            dma,
-            dma,
+            dma((2,)),
+            dma((2,)),
             dma((4,)),
             dma((4,)),
             pltpu.SemaphoreType.REGULAR,

time: 105 us -> 89.8 us (0.86)
  Pallas kernels: 98.2 us -> 82.6 us
    pallas_call x1, Pallas kernels: 91.9 us -> 76.3 us  [local(): pl.pallas_call(fused_kernel, out_shape=jax.ShapeDtypeStruct((4, DEVS, 16,...]
where the time goes in v3:
time: 89.8 us; the launch traced here: 89.4 us
  Pallas kernels  82.6 us (92%)
  other arithmetic  4.68 us (5%)
  local copies, waits for them, and re-layouts  2.06 us (2%)
    pallas_call x1, Pallas kernels, local(): pl.pallas_call(fused_kernel, out_shape=jax.ShapeDtypeStruct((4, DEVS, 16,...  76.3 us
    pallas_call x1, Pallas kernels, local(): pl.pallas_call(scatter_kernel, out_shape=jax.ShapeDtypeStruct(density.sha...  6.32 us

profile of v3, /device:TPU:1, one launch (start us, length us, event | category | flops | bytes accessed | tf_op | source)
XLA Modules:
  0.0 89.4 jit_solution(12395831756896378935)
XLA Ops:
  0.0 0.7 broadcast_compare_fusion.1
  0.7 0.2 select_reduce_fusion
  0.9 0.8 select_reduce_fusion.3
  1.7 0.5 convert_element_type.3.factor
  2.3 0.1 broadcast_in_dim.109
  2.3 0.1 broadcast_in_dim.110
  2.4 0.9 fusion.13
  3.3 0.8 fusion.14
  4.2 0.1 fusion.7
  4.3 0.2 select_reduce_fusion.2
  4.5 1.0 %select_reduce_fusion.1 = s32[128]{0:T(128)S(1)} fusion(s32[992]{0:T(1024)S(1)} %get-tuple-element.5, s32[992]{0:T(1024)} %param.8), kind=kLoop, calls=%fused_computation.3 | loop fusion | flops 380800 | bytes 8448 | tf_op jit(solution)/shard_map/reduce_sum | solution.py:368
  5.5 0.1 copy.6
  5.6 0.1 reshape.306.owners
  5.7 0.0 copy-start
  5.7 0.6 select_reduce_fusion.4.back
  6.3 0.5 add_maximum_fusion
  6.8 0.0 copy-done
  6.8 76.3 %fused.1.arrived = bf16[4,128,16,128]{3,2,1,0:T(8,128)(2,1)} custom-call(s32[128]{0:T(128)} %get-tuple-element.13.pick, s32[48]{0:T(128)} %copy-done, f32[8]{0:T(128)} %convert_element_type.3.factor, s32[128]{0:T(128)} %select_reduce_fusion.4.back, f32[16,8,8192]{2,1,0:T(8,128)} %dens_hbm.1, bf16[8,1024,1024]{2,1,0:T(8,128)(2,1)} %integ.1), custom_call_target="tpu_custom_call" | custom-call | tf_op jit(solution)/shard_map/fused/pallas_call | solution.py:400
  83.0 6.3 %scatter.1 = f32[16,8,8192]{2,1,0:T(8,128)} custom-call(s32[128]{0:T(128)} %get-tuple-element.14.table, bf16[4,128,16,128]{3,2,1,0:T(8,128)(2,1)} %fused.1.arrived), custom_call_target="tpu_custom_call" | custom-call | tf_op jit(solution)/shard_map/scatter/pallas_call | solution.py:433
  (4 shorter events, 0.1 us)
Async XLA Ops:
  5.7 1.1 %copy-start = (s32[48]{0:T(128)}, s32[48]{0:T(128)S(1)}, u32[]{:S(2)}) copy-start(s32[48]{0:T(128)S(1)} %reshape.306.owners) | copy-start | bytes 580

commit v4 on v3

--- a/solution.py
+++ b/solution.py
@@ -173,8 +173,49 @@
     return jnp.concatenate([x[c * 8 : (c + 1) * 8, :] for c in range(x.shape[0] // 8)], 1)
 
 
+def make_tables(data, tabs, facs):
+    r, c = here()
+    me = r * N_COL + c
+    first = [data[i : i + 1, :] for i in (0, 2, 0, 0, 1, 1)]
+    second = [data[i : i + 1, :] for i in (1, 3, 2, 3, 2, 3)]
+    holder = data[4:5, :]
+    owner = [f // ROWS_LOC * N_COL + s // COLS_LOC for f, s in zip(first, second)]
+    asked = jnp.zeros((1, 1024), jnp.int32)
+    for o, f, s in zip(owner, first, second):
+        asked += jnp.where((o == me) & (holder >= 0), f % ROWS_LOC * COLS_LOC + s % COLS_LOC + 1, 0)
+    dev = lax.broadcasted_iota(jnp.int32, (DEVS, 1024), 0)
+    hot = jnp.where(dev == holder, 1.0, 0.0).astype(BF16)
+    wanted = jnp.broadcast_to(asked.astype(F32), (8, 1024)).astype(BF16)
+    lid = lax.dot_general(wanted, hot, (((1,), (1,)), ((), ())), preferred_element_type=F32)[0:1].astype(jnp.int32)
+    own = jnp.broadcast_to(jnp.where(holder == me, 1, 0), (8, 1024))
+    lane = lax.broadcasted_iota(jnp.int32, (8, 1024), 1)
+    count = own
+    for shift in (1, 2, 4, 8, 16, 32, 64, 128, 256, 512):
+        count = count + jnp.where(lane >= shift, pltpu.roll(count, shift, 1), 0)
+    slot = lax.broadcasted_iota(jnp.int32, (8, 1024), 0)
+    sel = (own > 0) & (count - 1 == slot)
+    deg = jnp.sum(jnp.where(sel, data[5:6, :].astype(F32), 0.0), 1, keepdims=True)
+    col = lax.broadcasted_iota(jnp.int32, (8, DEVS), 1)
+    row = lax.broadcasted_iota(jnp.int32, (8, DEVS), 0)
+    owners = jnp.zeros((8, DEVS), F32)
+    back = jnp.zeros((8, DEVS), F32)
+    for t in range(6):
+        of = jnp.sum(jnp.where(sel, owner[t].astype(F32), 0.0), 1, keepdims=True)
+        owners = jnp.where(col == t, of, owners)
+        back += jnp.where((of == col.astype(F32)) & (deg > 0.0), (row * 6 + t).astype(F32), 0.0)
+    back = jnp.sum(back, 0, keepdims=True).astype(jnp.int32)
+    tabs[3:8, :] = jnp.zeros((5, DEVS), jnp.int32)
+    lid = jnp.clip(lid, 0, BLOCKS)
+    tabs[0:1, :] = jnp.maximum(lid - 1, 0)
+    tabs[1:2, :] = jnp.where(lid > 0, lid - 1, BLOCKS)
+    tabs[2:3, :] = jnp.clip(back, 0, 6 * SLOTS - 1)
+    tabs[8:16, :] = jnp.clip(owners.astype(jnp.int32), 0, DEVS - 1)
+    facs[...] = jnp.broadcast_to(deg, (8, DEVS))
+
+
 def fused_kernel(
-    pick, owners, factor, back, dens_hbm, integ, out,
+    data, dens_hbm, integ, out, tabs_out,
+    tabs_v, facs_v, tabs, facs, tab_sem,
     dens, a_all, g_all, work, send, recv0, recv1, give, d_nat, d_in, left, acc, o_acc, o_perm, perm, contrib,
     dens_sem, a_sem, send_sem, recv_sem, give_sem, back_sem, col_sem,
 ):
@@ -187,6 +228,10 @@
         return pltpu.make_async_copy(integ.at[q], a_all.at[q], a_sem.at[q])
 
     greet()
+    make_tables(data, tabs_v, facs_v)
+    tab_in = [pltpu.make_async_copy(tabs_v, tabs, tab_sem.at[0]), pltpu.make_async_copy(facs_v, facs, tab_sem.at[1])]
+    for copy in tab_in:
+        copy.start()
     flat = work.reshape(160 * 64, 128)
     for i in range(4):
         dens_in[i].wait()
@@ -203,8 +248,12 @@
         load(q).start()
     blocks = work.at[pl.ds(0, 144)].reshape(BLOCKS, PITCH, 128)
 
+    for copy in tab_in:
+        copy.wait()
+    tabs_out[...] = tabs_v[...]
+
     def choose(h, _):
-        block = blocks[pick[h]].astype(BF16)
+        block = blocks[tabs[0, h]].astype(BF16)
         send[0, h] = block[:32]
         send[1, h] = block[32:64]
         return 0
@@ -240,7 +289,7 @@
 
         def collect(q, _):
             for t in range(6):
-                d_nat[kh, q * 6 + t] = lanes_of(recv[kh][owners[q * 6 + t]].astype(F32))
+                d_nat[kh, q * 6 + t] = lanes_of(recv[kh][tabs[8 + q, t]].astype(F32))
             for n, t in enumerate((4, 2)):
                 d_in[pl.ds(pl.multiple_of((q * 2 + n) * 8, 8), 8), :] = d_nat[kh, q * 6 + t]
             return 0
@@ -283,8 +332,8 @@
     def quarter(qt, hf, first):
         def one(q, _):
             base = q * 6
-            coul = 2.0 * factor[q]
-            exch = -0.5 * factor[q]
+            coul = 2.0 * facs[q, 0]
+            exch = -0.5 * facs[q, 0]
             j_pq, j_rs = coulomb(1, q, qt)
             contrib[qt, base] = (coul * (acc[qt, base] + j_pq)).astype(BF16)
             contrib[qt, base + 1] = (coul * (acc[qt, base + 1] + j_rs)).astype(BF16)
@@ -312,7 +361,7 @@
 
         def place(i, _):
             for j in range(8):
-                give[qt, i * 8 + j] = contrib[qt, back[i * 8 + j]]
+                give[qt, i * 8 + j] = contrib[qt, tabs[2, i * 8 + j]]
             return 0
 
         lax.fori_loop(0, DEVS // 8, place, 0)
@@ -332,53 +381,39 @@
         done.wait_send()
 
 
-def scatter_kernel(table, arrived, out, acc):
+def scatter_kernel(tabs, arrived, out, land, acc, whole, in_sem, out_sem):
+    loads = [pltpu.make_async_copy(arrived.at[qt], land.at[qt], in_sem.at[qt]) for qt in range(4)]
+    stores = [pltpu.make_async_copy(whole.at[pl.ds(i * 4, 4)], out.at[pl.ds(i * 4, 4)], out_sem.at[i]) for i in range(4)]
+    for copy in loads:
+        copy.start()
+
     def clear(i, _):
         acc[pl.ds(i * PITCH, PITCH), :] = jnp.zeros((PITCH, 128), F32)
         return 0
 
-    lax.fori_loop(0, BLOCKS + 1, clear, 0)
+    lax.fori_loop(0, BLOCKS, clear, 0, unroll=4)
+    for copy in loads:
+        copy.wait()
 
     def add(h, _):
-        at = pl.multiple_of(table[h] * PITCH, 8)
-        for qt in range(4):
-            acc[pl.ds(at + qt * 16, 16), :] += arrived[qt, h].astype(F32)
-        return 0
-
-    lax.fori_loop(0, DEVS, add, 0)
-
-    def join(a, _):
-        for ck in range(64):
-            k, c = ck // 8, ck % 8
-            out[a, :, ck * 128 : (ck + 1) * 128] = acc[pl.ds(a * 8 * PITCH + c * 8 + k, 8, stride=PITCH), :]
-        return 0
-
-    lax.fori_loop(0, ROWS_LOC, join, 0)
-
-
-def tables(quartets, holder, degeneracy):
-    me = lax.axis_index("row") * N_COL + lax.axis_index("col")
-    q = quartets.T
-    first = jnp.stack([q[0], q[2], q[0], q[0], q[1], q[1]])
-    second = jnp.stack([q[1], q[3], q[2], q[3], q[2], q[3]])
-    owner = first // ROWS_LOC * N_COL + second // COLS_LOC
-    local = first % ROWS_LOC * COLS_LOC + second % COLS_LOC
-    asked = jnp.sum(jnp.where(owner == me, local + 1, 0), 0)
-    devs = jnp.arange(DEVS, dtype=jnp.int32)
-    lid = jnp.sum(jnp.where(holder[None, :] == devs[:, None], asked[None, :], 0), 1)
-    pick = jnp.maximum(lid - 1, 0)
-    target = jnp.where(lid > 0, lid - 1, BLOCKS)
-    own = holder == me
-    order = jnp.arange(holder.shape[0], dtype=jnp.int32)
-    rank = jnp.sum(jnp.where(own[None, :] & (order[None, :] < order[:, None]), 1, 0), 1)
-    sel = own[None, :] & (rank[None, :] == jnp.arange(SLOTS, dtype=jnp.int32)[:, None])
-    owners = jnp.sum(jnp.where(sel[:, None, :], owner[None], 0), 2)
-    deg = jnp.sum(jnp.where(sel, degeneracy[None, :], 0), 1)
-    live = (deg > 0)[:, None]
-    flat = jnp.where(live, owners, -1).reshape(-1)
-    ids = jnp.arange(48, dtype=jnp.int32)
-    back = jnp.sum(jnp.where(flat[None, :] == devs[:, None], ids[None, :], 0), 1)
-    return pick, target, owners.reshape(-1), deg.astype(F32), back
+        at = pl.multiple_of(tabs[1, h] * PITCH, 8)
+        more = jnp.concatenate([land[qt, h].astype(F32) for qt in range(4)], 0)
+        acc[pl.ds(at, 64), :] += more
+        return 0
+
+    lax.fori_loop(0, DEVS, add, 0, unroll=4)
+    for i in range(4):
+
+        def join(a, _):
+            for ck in range(64):
+                k, c = ck // 8, ck % 8
+                whole[a, :, ck * 128 : (ck + 1) * 128] = acc[pl.ds(a * 8 * PITCH + c * 8 + k, 8, stride=PITCH), :]
+            return 0
+
+        lax.fori_loop(i * 4, i * 4 + 4, join, 0)
+        stores[i].start()
+    for copy in stores:
+        copy.wait()
 
 
 def vspec():
@@ -394,15 +429,21 @@
 
 
 def local(density, integrals, quartets, holder, degeneracy):
-    pick, target, owners, factor, back = tables(quartets, holder, degeneracy)
+    data = jnp.concatenate([quartets.T, holder[None], degeneracy[None]], 0)
+    data = jnp.pad(data, ((0, 2), (0, 1024 - data.shape[1])), constant_values=-1)
     anyspec = pl.BlockSpec(memory_space=pl.ANY)
     dma = pltpu.SemaphoreType.DMA
-    arrived = pl.pallas_call(
+    arrived, tabs = pl.pallas_call(
         fused_kernel,
-        out_shape=jax.ShapeDtypeStruct((4, DEVS, 16, 128), BF16),
-        in_specs=[sspec(), sspec(), sspec(), sspec(), anyspec, anyspec],
-        out_specs=vspec(),
+        out_shape=[jax.ShapeDtypeStruct((4, DEVS, 16, 128), BF16), jax.ShapeDtypeStruct((16, DEVS), jnp.int32)],
+        in_specs=[vspec(), anyspec, anyspec],
+        out_specs=[vspec(), vspec()],
         scratch_shapes=[
+            VMEM((16, DEVS), jnp.int32),
+            VMEM((8, DEVS), F32),
+            SMEM((16, DEVS), jnp.int32),
+            SMEM((8, DEVS), F32),
+            dma((2,)),
             VMEM((ROWS_LOC, COLS_LOC, 8192), F32),
             VMEM((SLOTS, 1024, 1024), BF16),
             VMEM((SLOTS, 1024, 1024), BF16),
@@ -429,16 +470,22 @@
         ],
         compiler_params=params(collective_id=0, has_side_effects=True),
         name="fused",
-    )(pick, owners, factor, back, density, integrals)
+    )(data, density, integrals)
     return pl.pallas_call(
         scatter_kernel,
         out_shape=jax.ShapeDtypeStruct(density.shape, F32),
-        in_specs=[sspec(), vspec()],
-        out_specs=vspec(),
-        scratch_shapes=[VMEM(((BLOCKS + 1) * PITCH, 128), F32)],
+        in_specs=[sspec(), anyspec],
+        out_specs=anyspec,
+        scratch_shapes=[
+            VMEM((4, DEVS, 16, 128), BF16),
+            VMEM(((BLOCKS + 1) * PITCH, 128), F32),
+            VMEM(density.shape, F32),
+            dma((4,)),
+            dma((4,)),
+        ],
         compiler_params=params(),
         name="scatter",
-    )(target, arrived)
+    )(tabs, arrived)
 
 
 def solution(mesh):

time: 89.8 us -> 83.7 us (0.932)
  other arithmetic: 4.68 us -> 0.77 us
  local copies, waits for them, and re-layouts: 2.06 us -> 0.62 us
    reduce_sum x6 -> x0, other arithmetic: 2.92 us -> none  [the longest x1 1.03 us: tables(): jnp.sum(jnp.where(holder[None, :] == devs[:, None], asked[None, :], 0), 1)]
    slice x2 -> x0, local copies, waits for them, and re-layouts: 1.69 us -> none  [the longest x1 0.88 us: tables(): second = jnp.stack([q[1], q[3], q[2], q[3], q[2], q[3]])]
    pallas_call x1, Pallas kernels: 6.32 us -> 5.35 us  [local(): pl.pallas_call(scatter_kernel, out_shape=jax.ShapeDtypeStruct(density.sha...]
where the time goes in v4:
time: 83.7 us; the launch traced here: 83.4 us
  Pallas kernels  82 us (98%)
    pallas_call x1, Pallas kernels, local(): pl.pallas_call(fused_kernel, out_shape=[jax.ShapeDtypeStruct((4, DEVS, 16...  76.7 us
    pallas_call x1, Pallas kernels, local(): pl.pallas_call(scatter_kernel, out_shape=jax.ShapeDtypeStruct(density.sha...  5.35 us

profile of v4, /device:TPU:1, one launch (start us, length us, event | category | flops | bytes accessed | tf_op | source)
XLA Modules:
  0.0 83.4 jit_solution(89341897801299337)
XLA Ops:
  0.0 0.8 pad_add_fusion
  0.8 0.6 pad.4.data
  1.4 76.7 %fused.1 = (bf16[4,128,16,128]{3,2,1,0:T(8,128)(2,1)}, s32[16,128]{1,0:T(8,128)}) custom-call(s32[8,1024]{1,0:T(8,128)} %pad.4.data, f32[16,8,8192]{2,1,0:T(8,128)} %dens_hbm.1, bf16[8,1024,1024]{2,1,0:T(8,128)(2,1)} %integ.1), custom_call_target="tpu_custom_call" | custom-call | tf_op jit(solution)/shard_map/fused/pallas_call | solution.py:436
  78.1 5.3 %scatter.1 = f32[16,8,8192]{2,1,0:T(8,128)} custom-call(s32[16,128]{1,0:T(8,128)} %get-tuple-element.7.tabs, bf16[4,128,16,128]{3,2,1,0:T(8,128)(2,1)} %get-tuple-element.8.arrived), custom_call_target="tpu_custom_call" | custom-call | tf_op jit(solution)/shard_map/scatter/pallas_call | solution.py:474

commit v5 on v4

--- a/solution.py
+++ b/solution.py
@@ -214,8 +214,8 @@
 
 
 def fused_kernel(
-    data, dens_hbm, integ, out, tabs_out,
-    tabs_v, facs_v, tabs, facs, tab_sem,
+    quart, hold, degen, dens_hbm, integ, out, tabs_out,
+    data, tabs_v, facs_v, tabs, facs, tab_sem,
     dens, a_all, g_all, work, send, recv0, recv1, give, d_nat, d_in, left, acc, o_acc, o_perm, perm, contrib,
     dens_sem, a_sem, send_sem, recv_sem, give_sem, back_sem, col_sem,
 ):
@@ -228,6 +228,11 @@
         return pltpu.make_async_copy(integ.at[q], a_all.at[q], a_sem.at[q])
 
     greet()
+    count = hold.shape[1]
+    data[...] = jnp.full(data.shape, -1, jnp.int32)
+    data[0:4, :count] = quart[...]
+    data[4:5, :count] = hold[...]
+    data[5:6, :count] = degen[...]
     make_tables(data, tabs_v, facs_v)
     tab_in = [pltpu.make_async_copy(tabs_v, tabs, tab_sem.at[0]), pltpu.make_async_copy(facs_v, facs, tab_sem.at[1])]
     for copy in tab_in:
@@ -429,16 +434,15 @@
 
 
 def local(density, integrals, quartets, holder, degeneracy):
-    data = jnp.concatenate([quartets.T, holder[None], degeneracy[None]], 0)
-    data = jnp.pad(data, ((0, 2), (0, 1024 - data.shape[1])), constant_values=-1)
     anyspec = pl.BlockSpec(memory_space=pl.ANY)
     dma = pltpu.SemaphoreType.DMA
     arrived, tabs = pl.pallas_call(
         fused_kernel,
         out_shape=[jax.ShapeDtypeStruct((4, DEVS, 16, 128), BF16), jax.ShapeDtypeStruct((16, DEVS), jnp.int32)],
-        in_specs=[vspec(), anyspec, anyspec],
+        in_specs=[vspec(), vspec(), vspec(), anyspec, anyspec],
         out_specs=[vspec(), vspec()],
         scratch_shapes=[
+            VMEM((8, 1024), jnp.int32),
             VMEM((16, DEVS), jnp.int32),
             VMEM((8, DEVS), F32),
             SMEM((16, DEVS), jnp.int32),
@@ -470,7 +474,7 @@
         ],
         compiler_params=params(collective_id=0, has_side_effects=True),
         name="fused",
-    )(data, density, integrals)
+    )(quartets.T, holder[None], degeneracy[None], density, integrals)
     return pl.pallas_call(
         scatter_kernel,
         out_shape=jax.ShapeDtypeStruct(density.shape, F32),

time: 83.7 us -> 82.3 us (0.983)
  no operation moved by 1% of the time
where the time goes in v5:
time: 82.3 us; the launch traced here: 82 us
  Pallas kernels  82 us (100%)
    pallas_call x1, Pallas kernels, local(): pl.pallas_call(fused_kernel, out_shape=[jax.ShapeDtypeStruct((4, DEVS, 16...  76.7 us
    pallas_call x1, Pallas kernels, local(): pl.pallas_call(scatter_kernel, out_shape=jax.ShapeDtypeStruct(density.sha...  5.35 us

profile of v5, /device:TPU:1, one launch (start us, length us, event | category | flops | bytes accessed | tf_op | source)
XLA Modules:
  0.0 82.0 jit_solution(18038920090432458677)
XLA Ops:
  0.0 76.7 %fused.1 = (bf16[4,128,16,128]{3,2,1,0:T(8,128)(2,1)}, s32[16,128]{1,0:T(8,128)}) custom-call(s32[4,992]{1,0:T(4,128)} %bitcast.3, s32[1,992]{1,0:T(1,128)} %bitcast.4, s32[1,992]{1,0:T(1,128)} %bitcast.5, f32[16,8,8192]{2,1,0:T(8,128)} %dens_hbm.1, bf16[8,1024,1024]{2,1,0:T(8,128)(2,1)} %integ.1), custom_call_target="tpu_custom_call" | custom-call | tf_op jit(solution)/shard_map/fused/pallas_call | solution.py:439
  76.7 5.3 %scatter.1 = f32[16,8,8192]{2,1,0:T(8,128)} custom-call(s32[16,128]{1,0:T(8,128)} %get-tuple-element.7.tabs, bf16[4,128,16,128]{3,2,1,0:T(8,128)(2,1)} %get-tuple-element.8.arrived), custom_call_target="tpu_custom_call" | custom-call | tf_op jit(solution)/shard_map/scatter/pallas_call | solution.py:478

commit v6 on v5

--- a/solution.py
+++ b/solution.py
@@ -365,12 +365,23 @@
                 contrib[qt + 1, at] = two_rows(rows[:, 256:]).astype(BF16)
 
         def place(i, _):
-            for j in range(8):
-                give[qt, i * 8 + j] = contrib[qt, tabs[2, i * 8 + j]]
-            return 0
-
-        lax.fori_loop(0, DEVS // 8, place, 0)
-        post_all(give.at[qt], out.at[qt], give_sem.at[qt], back_sem.at[qt])
+            r, c = here()
+            tr = lax.rem(r + i, N_ROW)
+            ends = give.at[qt], out.at[qt], give_sem.at[qt], back_sem.at[qt]
+            for j in range(N_COL):
+                give[qt, tr * N_COL + j] = contrib[qt, tabs[2, tr * N_COL + j]]
+            for j in range(1, N_COL):
+                post(*ends, tr, lax.rem(c + j, N_COL))
+
+            @pl.when(i > 0)
+            def _():
+                post(*ends, tr, c)
+
+            return 0
+
+        lax.fori_loop(0, N_ROW, place, 0)
+        r, c = here()
+        out[qt, r * N_COL + c] = give[qt, r * N_COL + c]
 
     def half(hf, _):
         quarter(hf * 2, hf, True)

time: 82.3 us -> 81.7 us (level)
  no operation moved by 1% of the time
where the time goes in v6:
time: 81.7 us; the launch traced here: 81.5 us
  Pallas kernels  81.5 us (100%)
    pallas_call x1, Pallas kernels, local(): pl.pallas_call(fused_kernel, out_shape=[jax.ShapeDtypeStruct((4, DEVS, 16...  76.1 us
    pallas_call x1, Pallas kernels, local(): pl.pallas_call(scatter_kernel, out_shape=jax.ShapeDtypeStruct(density.sha...  5.36 us

profile of v6, /device:TPU:1, one launch (start us, length us, event | category | flops | bytes accessed | tf_op | source)
XLA Modules:
  0.0 81.5 jit_solution(13703243661995910285)
XLA Ops:
  0.0 76.1 %fused.1 = (bf16[4,128,16,128]{3,2,1,0:T(8,128)(2,1)}, s32[16,128]{1,0:T(8,128)}) custom-call(s32[4,992]{1,0:T(4,128)} %bitcast.3, s32[1,992]{1,0:T(1,128)} %bitcast.4, s32[1,992]{1,0:T(1,128)} %bitcast.5, f32[16,8,8192]{2,1,0:T(8,128)} %dens_hbm.1, bf16[8,1024,1024]{2,1,0:T(8,128)(2,1)} %integ.1), custom_call_target="tpu_custom_call" | custom-call | tf_op jit(solution)/shard_map/fused/pallas_call | solution.py:450
  76.1 5.4 %scatter.1 = f32[16,8,8192]{2,1,0:T(8,128)} custom-call(s32[16,128]{1,0:T(8,128)} %get-tuple-element.7.tabs, bf16[4,128,16,128]{3,2,1,0:T(8,128)(2,1)} %get-tuple-element.8.arrived), custom_call_target="tpu_custom_call" | custom-call | tf_op jit(solution)/shard_map/scatter/pallas_call | solution.py:489
